TPU v7x, 768 devices: a whole 4x8x12 slice. The times are simulated.
768 devices in a mesh: table: 64 (over y, x, core), rep: 12 (over z).
Axes of the slice: x: 4, y: 8, z: 12, core: 2. Of those that a mesh axis runs over, the one named last changes fastest.
Arguments:
- item_rows: float32 [196608, 64], P('table')
- row_accum: float32 [196608], P('table'), may hold values from 1e-06 to 0.0001
- w_query: float32 [64, 64], replicated
- w_hidden: float32 [192, 200], replicated, may hold values from -0.4375 to 0.4375
- w_logit: float32 [200], replicated, may hold values from -0.4375 to 0.4375
- wanted_rows: int32 [768, 64, 48], P(('table', 'rep')), may hold values from 0 to 3071, as said below
- behaviour_slots: int32 [6144, 1024], P(('table', 'rep')), may hold values from 0 to 3071, as said below
- target_slots: int32 [6144], P(('table', 'rep')), may hold values from 0 to 3071, as said below
- seq_lengths: int32 [6144], P(('table', 'rep')), may hold values from 32 to 1024
- clicks: int32 [6144], P(('table', 'rep')), may hold values 0 or 1
- fake_flags: int32 [6144], P(('table', 'rep')), may hold values 0 or 1
Outputs:
- new_rows: float32 [196608, 64], P('table')
- new_accum: float32 [196608], P('table')
- grad_query: float32 [64, 64], replicated
- grad_hidden: float32 [192, 200], replicated
- grad_logit: float32 [200], replicated
Inputs may be any that keep to these rules, and one draw needn't show every extreme that they name: `wanted_rows`: the 48 rows that one device asks of one owner are distinct, and entry k of such a list lies in rows k * (64) to (k + 1) * 64 - 1. `behaviour_slots`: slot s refers to entry s % 48 of the device's list for owner s // 48. `target_slots`: a slot as in behaviour_slots.
All inputs are finite; a program needn't handle non-finite values. No bound on the sum of `clicks` or of `fake_flags` on one device may be relied on, other than what follows from the above.
Results may differ from a plain program's by a relative error of at most 0.00035.
Values sent between devices are 32-bit elements; how exact they have to be, the bound alone decides.
A program may use at most 32 MiB of HBM per device.

v0:
```python
import jax
import jax.numpy as jnp
from jax import lax
from jax.sharding import PartitionSpec as P

FAKE_WEIGHT = 0.3
LEARN_RATE = 0.1


def forward_loss(keys, target, w_query, w_hidden, w_logit, seq_lengths, clicks, fake_flags):
    highest = lax.Precision.HIGHEST
    query = jnp.dot(target, w_query, precision=highest)
    scores = jnp.einsum("use,ue->us", keys, query, precision=highest) * keys.shape[2] ** (-0.5)
    valid = jnp.arange(keys.shape[1], dtype=jnp.int32)[None, :] < seq_lengths[:, None]
    largest = lax.stop_gradient(jnp.max(jnp.where(valid, scores, -1e30), axis=1, keepdims=True))
    raised = jnp.exp(jnp.where(valid, scores - largest, -1e30))
    weights = raised / jnp.sum(raised, axis=1, keepdims=True)
    pooled = jnp.einsum("us,use->ue", weights, keys, precision=highest)
    features = jnp.concatenate([pooled, target, pooled * target], axis=1)
    hidden = jax.nn.silu(jnp.dot(features, w_hidden, precision=highest))
    logit = jnp.dot(hidden, w_logit, precision=highest)
    labels_f = clicks.astype(logit.dtype)
    scale = jnp.where(clicks == 1, 1.0, jnp.where(fake_flags == 1, FAKE_WEIGHT, 1.0)).astype(
        logit.dtype
    )
    return jnp.sum(scale * (jax.nn.softplus(logit) - labels_f * logit))


def adagrad(rows_in, accum_in, grads):
    accum_out = accum_in + jnp.mean(grads * grads, axis=1)
    rows_out = rows_in - LEARN_RATE * grads / jnp.sqrt(accum_out)[:, None]
    return (rows_out, accum_out)


def local(
    item_rows,
    row_accum,
    w_query,
    w_hidden,
    w_logit,
    wanted_rows,
    behaviour_slots,
    target_slots,
    seq_lengths,
    clicks,
    fake_flags,
):
    width = item_rows.shape[1]
    owners = wanted_rows.shape[1]
    capacity = wanted_rows.shape[2]
    slot_count = owners * capacity
    asked = lax.all_to_all(wanted_rows[0], "table", split_axis=0, concat_axis=0, tiled=True)
    looked_up = item_rows[asked]
    arrived = lax.all_to_all(looked_up, "table", split_axis=0, concat_axis=0, tiled=True)
    slot_rows = arrived.reshape(slot_count, width)
    keys = slot_rows[behaviour_slots]
    target = slot_rows[target_slots]

    def local_loss(keys_in, target_in, query_in, hidden_in, logit_in):
        return forward_loss(
            keys_in, target_in, query_in, hidden_in, logit_in, seq_lengths, clicks, fake_flags
        )

    loss, pull = jax.vjp(local_loss, keys, target, w_query, w_hidden, w_logit)
    key_grad, target_grad, d_query, d_hidden, d_logit = pull(jnp.ones_like(loss))
    key_grad = key_grad.astype(jnp.bfloat16)
    slot_grad = jax.ops.segment_sum(
        key_grad.astype(jnp.float32).reshape(-1, width), behaviour_slots.reshape(-1), slot_count
    )
    slot_grad = slot_grad + jax.ops.segment_sum(target_grad, target_slots, slot_count)
    homed = lax.all_to_all(
        slot_grad.reshape(owners, capacity, width), "table", split_axis=0, concat_axis=0, tiled=True
    )
    grad_query, grad_hidden, grad_logit = lax.psum((d_query, d_hidden, d_logit), ("table", "rep"))
    row_grad = (
        jnp.zeros(item_rows.shape, jnp.float32).at[asked.reshape(-1)].add(homed.reshape(-1, width))
    )
    total = lax.psum(row_grad, "rep")
    new_rows, new_accum = adagrad(item_rows, row_accum, total)
    return (new_rows, new_accum, grad_query, grad_hidden, grad_logit)


def solution(mesh):
    in_specs = (
        P("table", None),
        P("table"),
        P(),
        P(),
        P(),
        P(("table", "rep"), None, None),
        P(("table", "rep"), None),
        P(("table", "rep")),
        P(("table", "rep")),
        P(("table", "rep")),
        P(("table", "rep")),
    )
    out_specs = (P("table", None), P("table"), P(), P(), P())
    return jax.shard_map(local, mesh=mesh, in_specs=in_specs, out_specs=out_specs, check_vma=False)
```

profile of v0, /device:TPU:24, one launch (start us, length us, event | category | flops | bytes accessed | tf_op | source)
XLA Modules:
  0.0 818.1 jit_solution(4687266549133966169)
XLA Ops:
  7.2 1.5 copy.26
  8.7 13.4 %all-to-all-start = ((s32[64,1,48]{2,1,0:T(1,128)}), s32[64,1,48]{2,1,0:T(1,128)S(1)}, u32[]{:S(2)}, u32[]{:S(2)}) async-start(s32[64,1,48]{2,1,0:T(1,128)} %bitcast), calls=%async_computation | async-start | bytes 65536 | tf_op jit(solution)/shard_map/all_to_all | solution.py:52
  22.1 1.6 copy.32
  23.7 5.2 all-to-all-done
  29.0 8.1 gather_fusion
  37.2 1.9 reshape.191
  39.0 7.3 all-to-all-start.1
  46.4 22.6 %all-to-all-done.1 = f32[64,1,3072]{2,1,0:T(1,128)S(1)} async-done(((f32[64,1,3072]{2,1,0:T(1,128)}), f32[64,1,3072]{2,1,0:T(1,128)S(1)}, u32[]{:S(2)}, u32[]{:S(2)}) %all-to-all-start.1) | async-done | bytes 786464 | tf_op jit(solution)/shard_map/all_to_all | solution.py:54
  69.0 0.5 broadcast.109
  69.5 3.6 reduce.4
  73.1 1.5 reshape.192
  74.6 0.6 gather_fusion.2
  75.2 27.7 %gather_fusion.1 = f32[8192,64]{1,0:T(8,128)} fusion(f32[3072,64]{1,0:T(8,128)S(1)} %bitcast.89, s32[8192]{0:T(1024)S(1)} %bitcast_clamp_fusion), kind=kCustom, calls=%fused_computation.1 | custom fusion | bytes 4227072 | tf_op jit(solution)/shard_map/gather | solution.py:56
  102.9 0.1 fusion.39
  103.1 6.0 fusion.40
  109.1 0.2 select_reduce_fusion
  109.3 0.2 fusion.37
  109.8 2.1 fusion.16
  111.9 0.2 fusion.22
  112.2 0.2 multiply_add_fusion.1
  112.3 0.3 fusion.35
  112.7 3.6 fusion.41
  116.2 0.2 fusion.13
  116.5 2.1 fusion.14
  118.6 0.2 convolution_add_fusion
  118.8 4.1 add_convert_fusion
  123.0 1.0 scatter_custom_fusion.1
  124.0 46.0 %scatter_custom_fusion = f32[3072,64]{1,0:T(8,128)} fusion(s32[8192]{0:T(1024)S(1)} %bitcast.109, bf16[8192,64]{1,0:T(8,128)(2,1)} %bitcast.94, f32[]{:T(128)} %constant.12.clone.1), kind=kCustom, calls=%fused_computation.6 | custom fusion | flops 1048576 | bytes 1835012 | tf_op jit(solution)/shard_map/scatter-add | solution.py:67
  170.0 2.7 add.72
  172.7 3.1 reshape.193
  175.8 6.3 all-to-all-start.2
  182.2 0.5 broadcast.106
  182.7 0.7 reduce.3
  183.5 21.3 %all-to-all-done.2 = f32[64,1,3072]{2,1,0:T(1,128)S(1)} async-done(((f32[64,1,3072]{2,1,0:T(1,128)}), f32[64,1,3072]{2,1,0:T(1,128)S(1)}, u32[]{:S(2)}, u32[]{:S(2)}) %all-to-all-start.2) | async-done | bytes 786464 | tf_op jit(solution)/shard_map/all_to_all | solution.py:71
  204.8 2.5 reduce.5
  207.3 1.6 reshape.194
  208.9 18.4 %scatter_custom_fusion.2 = f32[3072,64]{1,0:T(8,128)} fusion(s32[3072]{0:T(1024)S(1)} %bitcast.110, f32[3072,64]{1,0:T(8,128)} %bitcast.97, f32[]{:T(128)} %constant.12.clone.1), kind=kCustom, calls=%fused_computation.13 | custom fusion | flops 196608 | bytes 786944 | tf_op jit(solution)/shard_map/scatter-add | solution.py:76
  227.4 0.1 fusion.23
  227.5 0.2 fusion.42
  227.8 1.1 fusion.21
  228.9 111.3 %all-reduce = (f32[64,64]{1,0:T(8,128)}, f32[200]{0:T(256)}) all-reduce(f32[64,64]{1,0:T(8,128)S(1)} %fusion.42, f32[200]{0:T(256)S(1)} %bitcast.112), channel_id=1, replica_groups=mesh['table'=64,'rep'=12] {'table','rep'}, use_global_device_ids=true, to_apply=%region_8.9 | all-reduce | flops 4296 | bytes 34368 | tf_op jit(solution)/shard_map/psum | solution.py:74
  340.2 4.5 all-reduce.4.cloned.1.call-done
  344.7 2.0 multiply_reduce_fusion
  346.7 0.6 fusion.38
  347.3 0.5 divide_subtract_fusion
  347.9 1.3 copy.33
  349.2 460.4 %all-reduce.6.cloned.1.call-done = f32[192,200]{1,0:T(8,128)} async-done(((f32[192,200]{1,0:T(8,128)}), f32[192,200]{1,0:T(8,128)}) %all-reduce.6.cloned.1.call-update) | async-done | bytes 153616 | tf_op jit(solution)/shard_map/psum | solution.py:74
  809.6 1.6 copy.72
  (43 shorter events, 0.7 us)
Async XLA Ops:
  7.2 104.7 %copy-start = (f32[192,200]{1,0:T(8,128)S(1)}, f32[192,200]{1,0:T(8,128)}, u32[]{:S(2)}) copy-start(f32[192,200]{1,0:T(8,128)} %param.14) | copy-start | bytes 460804
  8.7 20.3 %all-to-all-start = ((s32[64,1,48]{2,1,0:T(1,128)}), s32[64,1,48]{2,1,0:T(1,128)S(1)}, u32[]{:S(2)}, u32[]{:S(2)}) async-start(s32[64,1,48]{2,1,0:T(1,128)} %bitcast), calls=%async_computation | async-start | bytes 65536 | tf_op jit(solution)/shard_map/all_to_all | solution.py:52
  37.1 9.2 %copy-start.4 = (s32[8,1024]{1,0:T(8,128)S(1)}, s32[8,1024]{1,0:T(8,128)}, u32[]{:S(2)}) copy-start(s32[8,1024]{1,0:T(8,128)} %param.17) | copy-start | bytes 98308
  37.1 9.2 %copy-start.10 = (s32[8]{0:T(128)S(1)}, s32[8]{0:T(128)}, u32[]{:S(2)}) copy-start(s32[8]{0:T(128)} %param.18) | copy-start | bytes 100
  39.0 30.0 %all-to-all-start.1 = ((f32[64,1,3072]{2,1,0:T(1,128)}), f32[64,1,3072]{2,1,0:T(1,128)S(1)}, u32[]{:S(2)}, u32[]{:S(2)}) async-start(f32[64,1,3072]{2,1,0:T(1,128)} %reshape.191), calls=%async_computation.1 | async-start | bytes 1572864 | tf_op jit(solution)/shard_map/all_to_all | solution.py:54
  75.2 27.7 %copy-start.3 = (f32[64,64]{1,0:T(8,128)S(1)}, f32[64,64]{1,0:T(8,128)}, u32[]{:S(2)}) copy-start(f32[64,64]{1,0:T(8,128)} %param.13) | copy-start | bytes 49156
  103.1 6.1 copy-start.5
  103.1 6.7 copy-start.1
  109.7 2.4 copy-start.7
  109.7 2.4 copy-start.8
  109.7 2.4 copy-start.9
  175.8 29.0 %all-to-all-start.2 = ((f32[64,1,3072]{2,1,0:T(1,128)}), f32[64,1,3072]{2,1,0:T(1,128)S(1)}, u32[]{:S(2)}, u32[]{:S(2)}) async-start(f32[64,1,3072]{2,1,0:T(1,128)} %reshape.193), calls=%async_computation.2 | async-start | bytes 1572864 | tf_op jit(solution)/shard_map/all_to_all | solution.py:71
  182.1 162.6 %all-reduce.4.cloned.1.call-start = ((), (), s32[]{:S(2)}) async-start(), calls=%async_computation.3 | async-start | bytes 3145728 | tf_op jit(solution)/shard_map/psum | solution.py:78
  227.3 119.4 %copy-start.6 = (f32[3072]{0:T(1024)S(1)}, f32[3072]{0:T(1024)}, u32[]{:S(2)}) copy-start(f32[3072]{0:T(1024)} %param.12) | copy-start | bytes 36868
  227.3 582.3 %all-reduce.6.cloned.1.call-start = ((), (), s32[]{:S(2)}) async-start(), calls=%async_computation.4 | async-start | bytes 393216 | tf_op jit(solution)/shard_map/psum | solution.py:74
  344.7 2.6 copy-start.2
Sparse Core Ops, SparseCore 0:
  227.5 117.2 all-reduce.3
  350.7 458.8 all-reduce.5
where the time goes:
time: 819 us; the launch traced here: 818 us
  waiting for transfers between devices  514 us (63%)
  blocking collectives  111 us (14%)
  other arithmetic  83.2 us (10%)
  local copies, waits for them, and re-layouts  51.7 us (6%)
  starting transfers between devices  27.1 us (3%)
  matrix products  16.3 us (2%)
  between operations  14.4 us (2%)
    psum x1, waiting for transfers between devices, local(): lax.psum((d_query, d_hidden, d_logit), ('table', 'rep'))  460 us
    psum x1, blocking collectives, local(): lax.psum((d_query, d_hidden, d_logit), ('table', 'rep'))  111 us
    scatter-add x1, other arithmetic, local(): jax.ops.segment_sum(key_grad.astype(jnp.float32).reshape(-1, width), beha...  46 us
    gather x1, local copies, waits for them, and re-layouts, local(): keys = slot_rows[behaviour_slots]  27.7 us
    all_to_all x1, waiting for transfers between devices, local(): lax.all_to_all(looked_up, 'table', split_axis=0, concat_axis=0, tiled=True)  22.6 us
    all_to_all x1, waiting for transfers between devices, local(): lax.all_to_all(slot_grad.reshape(owners, capacity, width), 'table', split...  21.3 us
    scatter-add x1, other arithmetic, local(): jnp.zeros(item_rows.shape, jnp.float32).at[asked.reshape(-1)]  18.4 us
  transfers between devices with their start and end apart: 5, of which 5 were waited for; matrix products, arithmetic and copies ran while one was open for 1% of the time, Pallas kernels for 0%

commit v1 on v0

v1 whole, which is shorter than its diff:
```python
import functools

import jax
import jax.numpy as jnp
from jax import lax
from jax.experimental import pallas as pl
from jax.experimental.pallas import tpu as pltpu
from jax.sharding import PartitionSpec as P

FAKE_WEIGHT = 0.3
LEARN_RATE = 0.1
MESH = pl.DeviceIdType.MESH
CORES, CHIPS_X = 2, 4
LANES = 128
E = 64
HID = 200
USERS = 8
PIECE = 24
F32, BF16 = jnp.float32, jnp.bfloat16


def iota(shape, dim):
    return lax.broadcasted_iota(jnp.int32, shape, dim)


def exact_dot(a, b, contract=((1,), (0,))):
    return lax.dot_general(
        a, b, (contract, ((), ())), precision=lax.Precision.HIGHEST, preferred_element_type=F32
    )


def bf16_dot(a, b, contract=((1,), (0,))):
    return lax.dot_general(a, b, (contract, ((), ())), preferred_element_type=F32)


def split3(x):
    high = x.astype(BF16)
    rest = x - high.astype(F32)
    middle = rest.astype(BF16)
    return high, middle, (rest - middle.astype(F32)).astype(BF16)


def column(ref):
    at = iota((USERS, 1), 0)
    out = jnp.zeros((USERS, 1), jnp.int32)
    for user in range(USERS):
        out = jnp.where(at == user, ref[user], out)
    return out


def place_of(slots, capacity):
    owner = lax.shift_right_logical(slots * 87382, 22)
    entry = slots - owner * capacity
    return owner * (capacity // 2) + lax.shift_right_logical(entry, 1), entry & 1


def sigmoid(x):
    return 1.0 / (1.0 + jnp.exp(-x))


def kernel(
    nt, nr, capacity,
    items, accum, w_query, w_hidden, w_logit, want, slots, targets, lengths, clicks, flags,
    out_rows, out_accum, out_query, out_hidden, out_logit,
    parts, asked_out, asked, onehot, looked, fetched, fetched_t, count, aimed, code_hi, code_lo,
    weight, dscore, cast, slot_grad, homed, index_t, named, sums_r, sums_l, got_r, got_l,
    weights, weights_z, weights_c, weights_x, weights_y, share,
    ask_sem, row_sem, grad_sem, wz_sem, wc_sem, wx_sem, wy_sem,
    rs_send_r, rs_recv_r, rs_send_l, rs_recv_l, ag_send_r, ag_recv_r, ag_send_l, ag_recv_l,
):
    me, rep = lax.axis_index("table"), lax.axis_index("rep")
    pairs = capacity // 2
    per_rep = pairs // nr
    columns = nt * pairs
    steps_r, steps_l = nr // 2, nr - 1 - nr // 2
    right, left = lax.rem(rep + 1, nr), lax.rem(rep + nr - 1, nr)

    def block(i):
        return pl.ds(pl.multiple_of(i * pairs, 8), pairs)

    def send(src, dst, sems, to):
        pltpu.make_async_remote_copy(
            src_ref=src, dst_ref=dst, send_sem=sems[0], recv_sem=sems[1], device_id=to, device_id_type=MESH
        ).start()

    def wait_bytes(ref, sem):
        pltpu.make_async_copy(ref, ref, sem).wait()

    barrier = pltpu.get_barrier_semaphore()

    @pl.loop(1, nt)
    def _(i):
        pl.semaphore_signal(barrier, inc=1, device_id={"table": lax.rem(me + i, nt)}, device_id_type=MESH)

    @pl.loop(1, nr)
    def _(i):
        pl.semaphore_signal(barrier, inc=1, device_id={"rep": lax.rem(rep + i, nr)}, device_id_type=MESH)

    wanted = jnp.concatenate([want[...], jnp.zeros((LANES - capacity, nt), jnp.int32)], axis=0)
    asked_out[...] = wanted.T.reshape(nt, 1, LANES)
    for p, part in enumerate(split3(items[...])):
        parts[p] = part
    pl.semaphore_wait(barrier, nt - 1 + nr - 1)

    pltpu.make_async_copy(asked_out.at[me], asked.at[me], ask_sem.at[1]).start()

    @pl.loop(1, nt)
    def _(i):
        to = lax.rem(me + i, nt)
        send(asked_out.at[to], asked.at[me], (ask_sem.at[0], ask_sem.at[1]), {"table": to})

    wait_bytes(asked, ask_sem.at[1])

    asked_t = jnp.concatenate([asked[...].reshape(nt, LANES), jnp.zeros((LANES - nt, LANES), jnp.int32)], axis=0).T
    first = iota((LANES, nt), 0)
    low_half = iota((E, LANES), 1) < E
    index_t[...] = asked_t.reshape(LANES, 1, LANES)

    @pl.loop(0, pairs)
    def _(k):
        at = first + k * LANES
        hot = (at == index_t[2 * k][:, 0:nt]) | (at == index_t[2 * k + 1][:, 0:nt])
        hot = hot.astype(F32).astype(BF16)
        onehot[k] = hot
        lhs = []
        for p in range(3):
            rows = parts[p, :, pl.ds(pl.multiple_of(k * LANES, LANES), LANES)]
            zero = jnp.zeros_like(rows)
            lhs += [jnp.where(low_half, rows, zero), jnp.where(low_half, zero, rows)]
        got = bf16_dot(jnp.concatenate(lhs, axis=0), hot)
        got = got[0:LANES] + got[LANES : 2 * LANES] + got[2 * LANES : 3 * LANES]
        looked[pl.ds(k, nt, stride=pairs), :] = got.T

    pltpu.make_async_copy(looked.at[block(me)], fetched.at[block(me)], row_sem.at[1]).start()

    @pl.loop(1, nt)
    def _(i):
        to = lax.rem(me + i, nt)
        send(looked.at[block(to)], fetched.at[block(me)], (row_sem.at[0], row_sem.at[1]), {"table": to})

    seq = slots.shape[1]
    place, half = place_of(slots[...], capacity)
    chunks = columns // LANES
    valid = iota((USERS, seq), 1) < column(lengths)
    code_hi[...] = jnp.where(valid, half * chunks + lax.shift_right_logical(place, 7), -1).reshape(USERS, 1, seq)
    code_lo[...] = (place & (LANES - 1)).reshape(USERS, 1, seq)

    @pl.loop(0, USERS)
    def _(user):
        hi = (iota((2 * chunks, seq), 0) == code_hi[user]).astype(F32).astype(BF16)
        lo = (iota((LANES, seq), 0) == code_lo[user]).astype(F32).astype(BF16)
        named[user] = bf16_dot(hi, lo, ((1,), (1,)))

    for h in range(2):
        for c in range(chunks):
            count[h * USERS : (h + 1) * USERS, c * LANES : (c + 1) * LANES] = named[:, h * chunks + c, :]

    target_place, target_half = place_of(column(targets), capacity)
    lane = iota((USERS, columns), 1)
    hit = lane == target_place
    for h in range(2):
        aimed[h * USERS : (h + 1) * USERS, :] = (hit & (target_half == h)).astype(F32)
    weights[...] = jnp.zeros_like(weights)

    wait_bytes(fetched, row_sem.at[1])

    @pl.loop(0, chunks)
    def _(c):
        at = pl.ds(pl.multiple_of(c * LANES, LANES), LANES)
        fetched_t[:, at] = fetched[at, :].T

    def fold(x):
        return x[0:USERS, 0:E] + x[USERS : 2 * USERS, E : 2 * E]

    def spread(x):
        zero = jnp.zeros_like(x)
        return jnp.concatenate(
            [jnp.concatenate([x, zero], axis=1), jnp.concatenate([zero, x], axis=1)], axis=0
        )

    def both(x):
        return jnp.concatenate([x, x], axis=0)

    rows = fetched[...]
    target = fold(exact_dot(aimed[...], rows))
    query = exact_dot(target, w_query[...]) * E ** (-0.5)
    scores = exact_dot(spread(query), fetched_t[...])
    times = count[...]
    present = times > 0.0
    scores = jnp.where(present, scores, -1e30)
    largest = jnp.max(scores, axis=1, keepdims=True)
    largest = both(jnp.maximum(largest[0:USERS], largest[USERS : 2 * USERS]))
    raised = jnp.where(present, jnp.exp(scores - largest), 0.0)
    total = jnp.sum(raised * times, axis=1, keepdims=True)
    total = both(total[0:USERS] + total[USERS : 2 * USERS])
    attention = raised / total
    weight[...] = attention
    pooled = fold(exact_dot(attention * times, rows))
    features = jnp.concatenate([pooled, target, pooled * target], axis=1)
    before = exact_dot(features, w_hidden[...])
    gate = sigmoid(before)
    hidden = before * gate
    logit = jnp.sum(hidden * w_logit[...], axis=1, keepdims=True)
    click = column(clicks)
    scale = jnp.where(click == 1, 1.0, jnp.where(column(flags) == 1, FAKE_WEIGHT, 1.0)).astype(F32)
    d_logit = scale * (sigmoid(logit) - click.astype(F32))
    d_before = d_logit * w_logit[...] * (gate + hidden * (1.0 - gate))
    weights[0 : 3 * E, 0:HID] = exact_dot(features.T, d_before)
    weights[4 * E : 4 * E + 1, 0:HID] = jnp.sum(hidden * d_logit, axis=0, keepdims=True)
    d_features = exact_dot(d_before, w_hidden[...], ((1,), (1,)))
    d_cross = d_features[:, 2 * E : 3 * E]
    d_pooled = d_features[:, 0:E] + d_cross * target
    d_target = d_features[:, E : 2 * E] + d_cross * pooled
    pull = exact_dot(spread(d_pooled), fetched_t[...])
    shift = jnp.sum(pooled * d_pooled, axis=1, keepdims=True)
    d_scores = attention * (pull - both(shift))
    dscore[...] = d_scores
    d_query = fold(exact_dot(d_scores * times, rows)) * E ** (-0.5)
    d_target = d_target + exact_dot(d_query, w_query[...], ((1,), (1,)))
    weights[3 * E : 4 * E, 0:E] = exact_dot(target.T, d_query)

    @pl.loop(1, nr)
    def _(i):
        to = lax.rem(rep + i, nr)
        piece = weights.at[pl.ds(pl.multiple_of(to * PIECE, 8), PIECE)]
        send(piece, weights_z.at[i - 1], (wz_sem.at[0], wz_sem.at[1]), {"rep": to})

    vectors = jnp.concatenate([d_pooled, query, d_target], axis=0)
    vectors = jnp.concatenate([vectors, jnp.zeros((3 * USERS, LANES - E), F32)], axis=1)
    vectors = jnp.concatenate([vectors, jnp.zeros((LANES - 3 * USERS, LANES), F32)], axis=0).T
    for i in range(3 * USERS):
        cast[i] = jnp.broadcast_to(vectors[0:E, i : i + 1], (E, LANES))

    @pl.loop(0, chunks)
    def _(c):
        at = pl.ds(pl.multiple_of(c * LANES, LANES), LANES)
        w_c, s_c, n_c, a_c = weight[:, at], dscore[:, at], count[:, at], aimed[:, at]
        halves = []
        for h in range(2):
            acc = jnp.zeros((E, LANES), F32)
            for u in range(USERS):
                row = slice(h * USERS + u, h * USERS + u + 1)
                key_grad = w_c[row] * cast[u] + s_c[row] * cast[USERS + u]
                key_grad = key_grad.astype(BF16).astype(F32)
                acc = acc + n_c[row] * key_grad + a_c[row] * cast[2 * USERS + u]
            halves.append(acc)
        slot_grad[at, :] = jnp.concatenate(halves, axis=0).T

    pltpu.make_async_copy(slot_grad.at[block(me)], homed.at[block(me)], grad_sem.at[1]).start()

    @pl.loop(1, nt)
    def _(i):
        to = lax.rem(me + i, nt)
        send(slot_grad.at[block(to)], homed.at[block(me)], (grad_sem.at[0], grad_sem.at[1]), {"table": to})

    wait_bytes(weights_z, wz_sem.at[1])
    piece = weights[pl.ds(pl.multiple_of(rep * PIECE, 8), PIECE), :]
    for i in range(nr - 1):
        piece = piece + weights_z[i]
    core = lax.rem(me, CORES)
    chip_x = lax.rem(lax.div(me, CORES), CHIPS_X)
    chip_y = lax.div(me, CORES * CHIPS_X)
    chips_y = nt // (CORES * CHIPS_X)

    def add_up(ref, count_of):
        out = ref[0]
        for i in range(1, count_of):
            out = out + ref[i]
        return out

    wait_bytes(homed, grad_sem.at[1])

    def send_cores():
        weights_c[core] = piece
        send(weights_c.at[core], weights_c.at[core], (wc_sem.at[0], wc_sem.at[1]), {"table": me + 1 - 2 * core})

    def send_x():
        wait_bytes(weights_c.at[0], wc_sem.at[1])
        weights_x[chip_x] = add_up(weights_c, CORES)

        @pl.loop(1, CHIPS_X)
        def _(i):
            to = lax.rem(chip_x + i, CHIPS_X)
            send(weights_x.at[chip_x], weights_x.at[chip_x], (wx_sem.at[0], wx_sem.at[1]),
                 {"table": (chip_y * CHIPS_X + to) * CORES + core})

    def send_y():
        wait_bytes(weights_x.at[pl.ds(0, CHIPS_X - 1)], wx_sem.at[1])
        weights_y[chip_y] = add_up(weights_x, CHIPS_X)

        @pl.loop(1, chips_y)
        def _(i):
            to = lax.rem(chip_y + i, chips_y)
            send(weights_y.at[chip_y], weights_y.at[chip_y], (wy_sem.at[0], wy_sem.at[1]),
                 {"table": (to * CHIPS_X + chip_x) * CORES + core})

    def own(dest, k):
        at = dest * per_rep + k
        parts_of = split3(homed[pl.ds(at, nt, stride=pairs), :])
        got = bf16_dot(onehot[at], jnp.concatenate(parts_of, axis=1))
        got = got[:, 0:LANES] + got[:, LANES : 2 * LANES] + got[:, 2 * LANES : 3 * LANES]
        return jnp.where(low_half, got[0:E], got[E : 2 * E])

    send_cores()
    for step in range(steps_r):
        for k in range(per_rep):
            dest = lax.rem(rep + steps_r - step, nr)
            value = own(dest, k)
            if step:
                wait_bytes(got_r.at[step - 1, k], rs_recv_r.at[step - 1, k])
                value = value + got_r[step - 1, k]
            sums_r[step, k] = value
            send(sums_r.at[step, k], got_r.at[step, k], (rs_send_r.at[step, k], rs_recv_r.at[step, k]), {"rep": right})
            if step < steps_l:
                dest = lax.rem(rep + nr - steps_l + step, nr)
                value = own(dest, k)
                if step:
                    wait_bytes(got_l.at[step - 1, k], rs_recv_l.at[step - 1, k])
                    value = value + got_l[step - 1, k]
                sums_l[step, k] = value
                send(sums_l.at[step, k], got_l.at[step, k], (rs_send_l.at[step, k], rs_recv_l.at[step, k]), {"rep": left})
        if step == 1:
            send_x()
        if step == 3:
            send_y()
    gradient = []
    for k in range(per_rep):
        value = own(rep, k)
        wait_bytes(got_l.at[steps_l - 1, k], rs_recv_l.at[steps_l - 1, k])
        value = value + got_l[steps_l - 1, k]
        wait_bytes(got_r.at[steps_r - 1, k], rs_recv_r.at[steps_r - 1, k])
        gradient.append(value + got_r[steps_r - 1, k])

    turned = jnp.concatenate(gradient, axis=0).T
    even, odd = turned[0:E], turned[E : 2 * E]
    blocks = [
        jnp.where(low_half, even, pltpu.roll(odd, E, 1)),
        jnp.where(low_half, pltpu.roll(even, E, 1), odd),
    ]
    for k in range(per_rep):
        at = rep * per_rep + k
        span = slice(k * LANES, (k + 1) * LANES)
        grads = blocks[k]
        new_accum = accum[at] + jnp.sum(grads * grads, axis=0, keepdims=True) * (1.0 / E)
        old = items[:, pl.ds(pl.multiple_of(at * LANES, LANES), LANES)]
        share[rep, 0:E, span] = old - LEARN_RATE * grads / jnp.sqrt(new_accum)
        share[rep, E : E + 8, span] = jnp.broadcast_to(new_accum, (8, LANES))
    wait_bytes(weights_y.at[pl.ds(0, chips_y - 1)], wy_sem.at[1])
    share[rep, E + 8 : E + 8 + PIECE, :] = add_up(weights_y, chips_y)

    cut = (E + 8 + PIECE) // 2
    spans = [pl.ds(0, cut), pl.ds(cut, cut)]

    def place(r):
        for k in range(per_rep):
            span = slice(k * LANES, (k + 1) * LANES)
            at = r * per_rep + k
            out_rows[:, pl.ds(pl.multiple_of(at * LANES, LANES), LANES)] = share[r, 0:E, span]
            out_accum[at] = share[r, E : E + 1, span]

    for step in range(steps_r):
        for k in range(2):
            source = lax.rem(rep + nr - step, nr)
            if step:
                wait_bytes(share.at[source, spans[k]], ag_recv_r.at[step - 1, k])
            part = share.at[source, spans[k]]
            send(part, part, (ag_send_r.at[step, k], ag_recv_r.at[step, k]), {"rep": right})
            if step < steps_l:
                source = lax.rem(rep + step, nr)
                if step:
                    wait_bytes(share.at[source, spans[k]], ag_recv_l.at[step - 1, k])
                part = share.at[source, spans[k]]
                send(part, part, (ag_send_l.at[step, k], ag_recv_l.at[step, k]), {"rep": left})
        place(lax.rem(rep + nr - step, nr))
        if 0 < step < steps_l:
            place(lax.rem(rep + step, nr))
    for k in range(2):
        source = lax.rem(rep + steps_l, nr)
        wait_bytes(share.at[source, spans[k]], ag_recv_l.at[steps_l - 1, k])
        source = lax.rem(rep + nr - steps_r, nr)
        wait_bytes(share.at[source, spans[k]], ag_recv_r.at[steps_r - 1, k])
    place(lax.rem(rep + steps_l, nr))
    place(lax.rem(rep + nr - steps_r, nr))

    flat = share[:, E + 8 : E + 8 + PIECE, :].reshape(nr * PIECE, 2 * LANES)
    out_hidden[...] = flat[0 : 3 * E, 0:HID]
    out_query[...] = flat[3 * E : 4 * E, 0:E]
    out_logit[...] = flat[4 * E : 4 * E + 1, 0:HID]

    wait_bytes(asked.at[pl.ds(0, nt - 1)], ask_sem.at[0])
    wait_bytes(looked.at[pl.ds(0, (nt - 1) * pairs)], row_sem.at[0])
    wait_bytes(slot_grad.at[pl.ds(0, (nt - 1) * pairs)], grad_sem.at[0])
    wait_bytes(weights_z, wz_sem.at[0])
    wait_bytes(weights_c.at[0], wc_sem.at[0])
    wait_bytes(weights_x.at[pl.ds(0, CHIPS_X - 1)], wx_sem.at[0])
    wait_bytes(weights_y.at[pl.ds(0, chips_y - 1)], wy_sem.at[0])
    for step in range(steps_r):
        for k in range(per_rep):
            wait_bytes(sums_r.at[step, k], rs_send_r.at[step, k])
            if step < steps_l:
                wait_bytes(sums_l.at[step, k], rs_send_l.at[step, k])
        for k in range(2):
            wait_bytes(share.at[0, spans[k]], ag_send_r.at[step, k])
            if step < steps_l:
                wait_bytes(share.at[0, spans[k]], ag_send_l.at[step, k])


def local(
    nt, nr, item_rows, row_accum, w_query, w_hidden, w_logit, wanted_rows, behaviour_slots,
    target_slots, seq_lengths, clicks, fake_flags,
):
    rows = item_rows.shape[0]
    capacity = wanted_rows.shape[2]
    pairs = capacity // 2
    columns = nt * pairs
    seq = behaviour_slots.shape[1]
    steps_r, steps_l = nr // 2, nr - 1 - nr // 2
    per_rep = pairs // nr
    vmem = pl.BlockSpec(memory_space=pltpu.VMEM)
    smem = pl.BlockSpec(memory_space=pltpu.SMEM)
    dma = pltpu.SemaphoreType.DMA
    wide = 2 * LANES
    scratch = [
        pltpu.VMEM((3, E, rows), BF16),
        pltpu.VMEM((nt, 1, LANES), jnp.int32),
        pltpu.VMEM((nt, 1, LANES), jnp.int32),
        pltpu.VMEM((pairs, LANES, nt), BF16),
        pltpu.VMEM((columns, LANES), F32),
        pltpu.VMEM((columns, LANES), F32),
        pltpu.VMEM((LANES, columns), F32),
        pltpu.VMEM((2 * USERS, columns), F32),
        pltpu.VMEM((2 * USERS, columns), F32),
        pltpu.VMEM((USERS, 1, seq), jnp.int32),
        pltpu.VMEM((USERS, 1, seq), jnp.int32),
        pltpu.VMEM((2 * USERS, columns), F32),
        pltpu.VMEM((2 * USERS, columns), F32),
        pltpu.VMEM((3 * USERS, E, LANES), F32),
        pltpu.VMEM((columns, LANES), F32),
        pltpu.VMEM((columns, LANES), F32),
        pltpu.VMEM((LANES, 1, LANES), jnp.int32),
        pltpu.VMEM((USERS, 2 * columns // LANES, LANES), F32),
        pltpu.VMEM((steps_r, per_rep, E, LANES), F32),
        pltpu.VMEM((steps_l, per_rep, E, LANES), F32),
        pltpu.VMEM((steps_r, per_rep, E, LANES), F32),
        pltpu.VMEM((steps_l, per_rep, E, LANES), F32),
        pltpu.VMEM((nr * PIECE, wide), F32),
        pltpu.VMEM((nr - 1, PIECE, wide), F32),
        pltpu.VMEM((CORES, PIECE, wide), F32),
        pltpu.VMEM((CHIPS_X, PIECE, wide), F32),
        pltpu.VMEM((nt // (CORES * CHIPS_X), PIECE, wide), F32),
        pltpu.VMEM((nr, E + 8 + PIECE, wide), F32),
        dma((2,)), dma((2,)), dma((2,)), dma((2,)), dma((2,)), dma((2,)), dma((2,)),
        dma((steps_r, per_rep)), dma((steps_r, per_rep)), dma((steps_l, per_rep)), dma((steps_l, per_rep)),
        dma((steps_r, 2)), dma((steps_r, 2)), dma((steps_l, 2)), dma((steps_l, 2)),
    ]
    new_rows, new_accum, grad_query, grad_hidden, grad_logit = pl.pallas_call(
        functools.partial(kernel, nt, nr, capacity),
        out_shape=(
            jax.ShapeDtypeStruct((E, rows), F32),
            jax.ShapeDtypeStruct((rows // LANES, 1, LANES), F32),
            jax.ShapeDtypeStruct((E, E), F32),
            jax.ShapeDtypeStruct((3 * E, HID), F32),
            jax.ShapeDtypeStruct((1, HID), F32),
        ),
        in_specs=[vmem] * 7 + [smem] * 4,
        out_specs=[vmem] * 5,
        scratch_shapes=scratch,
        compiler_params=pltpu.CompilerParams(
            collective_id=0, has_side_effects=True, vmem_limit_bytes=48 * 1024 * 1024
        ),
    )(
        item_rows.T,
        row_accum.reshape(rows // LANES, 1, LANES),
        w_query,
        w_hidden,
        w_logit.reshape(1, HID),
        wanted_rows[0].T,
        behaviour_slots,
        target_slots,
        seq_lengths,
        clicks,
        fake_flags,
    )
    return (new_rows.T, new_accum.reshape(rows), grad_query, grad_hidden, grad_logit.reshape(HID))


def solution(mesh):
    in_specs = (
        P("table", None),
        P("table"),
        P(),
        P(),
        P(),
        P(("table", "rep"), None, None),
        P(("table", "rep"), None),
        P(("table", "rep")),
        P(("table", "rep")),
        P(("table", "rep")),
        P(("table", "rep")),
    )
    out_specs = (P("table", None), P("table"), P(), P(), P())
    return jax.shard_map(
        functools.partial(local, mesh.shape["table"], mesh.shape["rep"]),
        mesh=mesh, in_specs=in_specs, out_specs=out_specs, check_vma=False,
    )
```

time: 819 us -> 135 us (0.16)
  the two profiles are of different devices: /device:TPU:24 before, /device:TPU:16 now
where the time goes in v1:
time: 135 us
  Pallas kernels  125 us (93%)
  local copies, waits for them, and re-layouts  9.04 us (7%)
    pallas_call x1, Pallas kernels, local(): pl.pallas_call(functools.partial(kernel, nt, nr, capacity), out_shape=(ja...  125 us
    unnamed x27, local copies, waits for them, and re-layouts  9.04 us

profile of v1, /device:TPU:16, one launch (start us, length us, event | category | flops | bytes accessed | tf_op | source)
XLA Modules:
  0.0 134.6 jit_solution(16935801352232587617)
XLA Ops:
  0.6 0.0 copy-start.8
  0.6 0.0 copy-start.9
  0.7 0.0 copy-start.10
  0.7 0.0 copy-start.6
  0.7 0.0 copy-start.7
  0.7 0.6 copy-done.8
  1.3 0.0 copy-done.9
  1.3 0.0 copy-done.10
  1.3 0.0 copy-done.6
  1.4 0.0 copy-done.7
  1.4 0.0 copy-start
  1.4 1.1 copy-done
  2.5 0.0 copy-start.1
  2.5 0.9 copy-done.1
  3.4 0.0 copy-start.2
  3.4 0.8 copy-done.2
  4.2 0.0 copy-start.3
  4.2 0.8 copy-done.3
  4.9 0.0 copy-start.4
  4.9 0.7 copy-done.4
  5.7 0.0 copy-start.5
  5.7 0.7 copy-done.5
  6.4 124.9 %shard_map.146 = (f32[64,3072]{1,0:T(8,128)S(1)}, f32[24,1,128]{2,1,0:T(1,128)S(1)}, f32[64,64]{1,0:T(8,128)S(1)}, f32[192,200]{1,0:T(8,128)S(1)}, f32[1,200]{1,0:T(1,128)S(1)}) custom-call(f32[64,3072]{1,0:T(8,128)S(1)} %bitcast.9, f32[24,1,128]{2,1,0:T(1,128)S(1)} %bitcast.12, f32[64,64]{1,0:T(8,128)S(1)} %copy-done.2, f32[192,200]{1,0:T(8,128)S(1)} %copy-done.1, ...), custom_call_target="tpu_custom_call" | custom-call | tf_op jit(solution)/shard_map/pallas_call | solution.py:456
  131.3 0.9 copy.21
  132.2 0.6 copy.22
  132.8 0.6 copy.23
  133.4 0.7 copy.24
  134.0 0.6 copy.25
Async XLA Ops:
  0.6 0.7 copy-start.8
  0.6 0.7 copy-start.9
  0.7 0.7 copy-start.10
  0.7 0.7 copy-start.6
  0.7 0.7 copy-start.7
  1.4 1.1 copy-start
  2.5 0.9 copy-start.1
  3.4 0.8 copy-start.2
  4.2 0.8 copy-start.3
  4.9 0.7 copy-start.4
  5.7 0.7 copy-start.5

commit v2 on v1

v2 whole, which is shorter than its diff:
```python
import functools

import jax
import jax.numpy as jnp
from jax import lax
from jax.experimental import pallas as pl
from jax.experimental.pallas import tpu as pltpu
from jax.sharding import PartitionSpec as P

FAKE_WEIGHT = 0.3
LEARN_RATE = 0.1
MESH = pl.DeviceIdType.MESH
CORES, CHIPS_X = 2, 4
LANES = 128
E = 64
HID = 200
USERS = 8
PIECE = 16
VMEM = 65000000
F32, BF16 = jnp.float32, jnp.bfloat16


def iota(shape, dim):
    return lax.broadcasted_iota(jnp.int32, shape, dim)


def exact_dot(a, b, contract=((1,), (0,))):
    return lax.dot_general(
        a, b, (contract, ((), ())), precision=lax.Precision.HIGHEST, preferred_element_type=F32
    )


def bf16_dot(a, b, contract=((1,), (0,))):
    return lax.dot_general(a, b, (contract, ((), ())), preferred_element_type=F32)


def split3(x):
    high = x.astype(BF16)
    rest = x - high.astype(F32)
    middle = rest.astype(BF16)
    return high, middle, (rest - middle.astype(F32)).astype(BF16)


def column(ref):
    at = iota((USERS, 1), 0)
    out = jnp.zeros((USERS, 1), jnp.int32)
    for user in range(USERS):
        out = jnp.where(at == user, ref[user], out)
    return out


def place_of(slots, capacity):
    owner = lax.shift_right_logical(slots * 87382, 22)
    entry = slots - owner * capacity
    k = lax.shift_right_logical(entry, 1) & 1
    return owner * (capacity // 2) + k * (capacity // 4) + lax.shift_right_logical(entry, 2), entry & 1


def early_rows(pairs):
    return -(-(pairs // 2) // 8) * 8


def sigmoid(x):
    return 1.0 / (1.0 + jnp.exp(-x))


def kernel(
    nt, nr, capacity,
    items_hbm, accum_hbm, w_query_hbm, w_hidden_hbm, w_logit_hbm, want_hbm, slots_hbm,
    targets_hbm, lengths_hbm, clicks_hbm, flags_hbm,
    out_rows, out_accum, out_query, out_hidden, out_logit,
    items, accum, w_query, w_hidden, w_logit, want, slots, targets, lengths, clicks, flags,
    parts, asked_out, asked, onehot, looked, fetched, fetched_t, count, aimed, code_hi, code_lo,
    weight, dscore, cast, slot_grad, homed_a, homed_b, index_t, named, sums, got,
    weights, weights_z, weights_c, weights_x, weights_y, cuts, spread_out, joined, whole, share,
    in_sem, ask_sem, row_sem, grad_sem, wz_sem, wc_sem, wx_sem, wy_sem, ws_sem, wj_sem, rs_send, rs_recv, ag_send, ag_recv,
):
    me, rep = lax.axis_index("table"), lax.axis_index("rep")
    pairs = capacity // 2
    per_rep = pairs // nr
    columns = nt * pairs
    rows = items_hbm.shape[1]

    def at_rep(distance):
        return lax.rem(rep + nr + distance, nr)

    def block(i):
        return pl.ds(pl.multiple_of(i * pairs, 8), pairs)

    def send(src, dst, sems, to):
        pltpu.make_async_remote_copy(
            src_ref=src, dst_ref=dst, send_sem=sems[0], recv_sem=sems[1], device_id=to, device_id_type=MESH
        ).start()

    def wait_bytes(ref, sem):
        pltpu.make_async_copy(ref, ref, sem).wait()

    drains = []
    brought = [
        pltpu.make_async_copy(src, dst, in_sem.at[i])
        for i, (src, dst) in enumerate([
            (want_hbm, want), (items_hbm, items), (slots_hbm, slots), (lengths_hbm, lengths), (targets_hbm, targets),
            (clicks_hbm, clicks), (flags_hbm, flags), (accum_hbm, accum), (w_query_hbm, w_query),
            (w_hidden_hbm, w_hidden), (w_logit_hbm, w_logit),
        ])
    ]
    brought[0].start()
    core = lax.rem(me, CORES)
    chip_x = lax.rem(lax.div(me, CORES), CHIPS_X)
    chip_y = lax.div(me, CORES * CHIPS_X)
    row = CORES * CHIPS_X
    chips_y = nt // row

    def device(y, x, c):
        return (lax.rem(y, chips_y) * CHIPS_X + lax.rem(x, CHIPS_X)) * CORES + lax.rem(c, CORES)

    def partner(j):
        m = lax.rem(j, chips_y)
        n = lax.rem(lax.div(j, chips_y) + 1, row)
        down, step = lax.rem(m, 2), lax.div(m, 2)
        dy = (chips_y // 2 - step) * (1 - down) + lax.rem(chips_y // 2 + 1 + step, chips_y) * down
        return device(chip_y + dy, chip_x + lax.div(n, CORES), core + lax.rem(n, CORES))

    barrier = pltpu.get_barrier_semaphore()

    @pl.loop(1, nt)
    def _(i):
        pl.semaphore_signal(barrier, inc=1, device_id={"table": lax.rem(me + i, nt)}, device_id_type=MESH)

    @pl.loop(1, nr)
    def _(i):
        pl.semaphore_signal(barrier, inc=1, device_id={"rep": lax.rem(rep + i, nr)}, device_id_type=MESH)

    for copy in brought[1:]:
        copy.start()
    brought[0].wait()
    wanted = jnp.concatenate([want[...], jnp.zeros((LANES - capacity, nt), jnp.int32)], axis=0)
    asked_out[...] = wanted.T.reshape(nt, 1, LANES)
    pl.semaphore_wait(barrier, nt - 1 + nr - 1)

    pltpu.make_async_copy(asked_out.at[me], asked.at[me], ask_sem.at[1]).start()

    @pl.loop(1, nt)
    def _(i):
        to = lax.rem(me + i, nt)
        send(asked_out.at[to], asked.at[me], (ask_sem.at[0], ask_sem.at[1]), {"table": to})

    drains.append((asked.at[pl.ds(0, nt - 1)], ask_sem.at[0]))
    for copy in brought[1:]:
        copy.wait()
    low_half = iota((E, LANES), 1) < E
    wide_low = (iota((E, rows), 1) & (LANES - 1)) < E
    for p, part in enumerate(split3(items[...])):
        part = part.astype(F32)
        parts[p * LANES : p * LANES + E, :] = jnp.where(wide_low, part, 0.0).astype(BF16)
        parts[p * LANES + E : (p + 1) * LANES, :] = jnp.where(wide_low, 0.0, part).astype(BF16)

    seq = slots.shape[1]
    place, half = place_of(slots[...], capacity)
    chunks = columns // LANES
    valid = iota((USERS, seq), 1) < column(lengths)
    code_hi[...] = jnp.where(valid, half * chunks + lax.shift_right_logical(place, 7), -1).reshape(USERS, 1, seq)
    code_lo[...] = (place & (LANES - 1)).reshape(USERS, 1, seq)

    @pl.loop(0, USERS)
    def _(user):
        hi = (iota((2 * chunks, seq), 0) == code_hi[user]).astype(F32).astype(BF16)
        lo = (iota((LANES, seq), 0) == code_lo[user]).astype(F32).astype(BF16)
        named[user] = bf16_dot(hi, lo, ((1,), (1,)))

    for h in range(2):
        for c in range(chunks):
            count[h * USERS : (h + 1) * USERS, c * LANES : (c + 1) * LANES] = named[:, h * chunks + c, :]

    target_place, target_half = place_of(column(targets), capacity)
    lane = iota((USERS, columns), 1)
    hit = lane == target_place
    for h in range(2):
        aimed[h * USERS : (h + 1) * USERS, :] = (hit & (target_half == h)).astype(F32)
    weights[:, LANES : 2 * LANES] = jnp.zeros((3 * E, LANES), F32)

    wait_bytes(asked, ask_sem.at[1])

    asked_t = jnp.concatenate([asked[...].reshape(nt, LANES), jnp.zeros((LANES - nt, LANES), jnp.int32)], axis=0).T
    first = iota((LANES, nt), 0)
    index_t[...] = asked_t.reshape(LANES, 1, LANES)

    @pl.loop(0, pairs, unroll=8)
    def _(p):
        k = per_rep * p - (per_rep * nr - 1) * lax.div(p, nr)
        at = first + k * LANES
        hot = (at == index_t[2 * k][:, 0:nt]) | (at == index_t[2 * k + 1][:, 0:nt])
        hot = hot.astype(F32).astype(BF16)
        onehot[p] = hot
        found = bf16_dot(parts[:, pl.ds(pl.multiple_of(k * LANES, LANES), LANES)], hot)
        found = found[0:LANES] + found[LANES : 2 * LANES] + found[2 * LANES : 3 * LANES]
        looked[pl.ds(p, nt, stride=pairs), :] = found.T

    pltpu.make_async_copy(looked.at[block(me)], fetched.at[block(me)], row_sem.at[1]).start()

    @pl.loop(0, nt - 1)
    def _(j):
        to = partner(j)
        send(looked.at[block(to)], fetched.at[block(me)], (row_sem.at[0], row_sem.at[1]), {"table": to})

    drains.append((looked.at[pl.ds(0, (nt - 1) * pairs)], row_sem.at[0]))
    wait_bytes(fetched, row_sem.at[1])

    @pl.loop(0, chunks)
    def _(c):
        at = pl.ds(pl.multiple_of(c * LANES, LANES), LANES)
        fetched_t[:, at] = fetched[at, :].T

    def fold(x):
        return x[0:USERS, 0:E] + x[USERS : 2 * USERS, E : 2 * E]

    def spread(x):
        zero = jnp.zeros_like(x)
        return jnp.concatenate(
            [jnp.concatenate([x, zero], axis=1), jnp.concatenate([zero, x], axis=1)], axis=0
        )

    def both(x):
        return jnp.concatenate([x, x], axis=0)

    keys = fetched[...]
    target = fold(exact_dot(aimed[...], keys))
    query = exact_dot(target, w_query[...]) * E ** (-0.5)
    scores = exact_dot(spread(query), fetched_t[...])
    times = count[...]
    present = times > 0.0
    scores = jnp.where(present, scores, -1e30)
    largest = jnp.max(scores, axis=1, keepdims=True)
    largest = both(jnp.maximum(largest[0:USERS], largest[USERS : 2 * USERS]))
    raised = jnp.where(present, jnp.exp(scores - largest), 0.0)
    total = jnp.sum(raised * times, axis=1, keepdims=True)
    total = both(total[0:USERS] + total[USERS : 2 * USERS])
    attention = raised / total
    weight[...] = attention
    pooled = fold(exact_dot(attention * times, keys))
    features = jnp.concatenate([pooled, target, pooled * target], axis=1)
    before = exact_dot(features, w_hidden[...])
    gate = sigmoid(before)
    hidden = before * gate
    logit = jnp.sum(hidden * w_logit[...], axis=1, keepdims=True)
    click = column(clicks)
    scale = jnp.where(click == 1, 1.0, jnp.where(column(flags) == 1, FAKE_WEIGHT, 1.0)).astype(F32)
    d_logit = scale * (sigmoid(logit) - click.astype(F32))
    d_before = d_logit * w_logit[...] * (gate + hidden * (1.0 - gate))
    weights[:, 0:HID] = exact_dot(features.T, d_before)
    d_w_logit = jnp.sum(hidden * d_logit, axis=0, keepdims=True)
    d_features = exact_dot(d_before, w_hidden[...], ((1,), (1,)))
    d_cross = d_features[:, 2 * E : 3 * E]
    d_pooled = d_features[:, 0:E] + d_cross * target
    d_target = d_features[:, E : 2 * E] + d_cross * pooled
    pull = exact_dot(spread(d_pooled), fetched_t[...])
    shift = jnp.sum(pooled * d_pooled, axis=1, keepdims=True)
    d_scores = attention * (pull - both(shift))
    dscore[...] = d_scores
    d_query = fold(exact_dot(d_scores * times, keys)) * E ** (-0.5)
    d_target = d_target + exact_dot(d_query, w_query[...], ((1,), (1,)))
    d_w_query = exact_dot(target.T, d_query)
    spare = HID - LANES
    room = LANES - spare
    low = jnp.concatenate([d_w_query, jnp.zeros((E, LANES - E), F32)], axis=1)
    row_a = d_w_logit[:, 0:LANES]
    row_b = jnp.concatenate([d_w_logit[:, LANES:HID], jnp.zeros((1, room), F32)], axis=1)
    logit_rows = [
        pltpu.roll(row_a, spare, 1), pltpu.roll(row_a, spare - room, 1), pltpu.roll(row_a, spare + LANES - 2 * room, 1),
        pltpu.roll(row_b, spare, 1), pltpu.roll(row_b, spare - room, 1), jnp.zeros((E - 5, LANES), F32),
    ]
    extra = [pltpu.roll(low, spare, 1), pltpu.roll(low, spare - room, 1)] + logit_rows
    second = weights[:, LANES : 2 * LANES]
    free = iota((3 * E, LANES), 1) >= spare
    weights[:, LANES : 2 * LANES] = jnp.where(free, jnp.concatenate(extra, axis=0), second)

    @pl.loop(1, nr)
    def _(i):
        to = lax.rem(rep + i, nr)
        piece = weights.at[pl.ds(pl.multiple_of(to * PIECE, 8), PIECE)]
        send(piece, weights_z.at[i - 1], (wz_sem.at[0], wz_sem.at[1]), {"rep": to})

    drains.append((weights_z, wz_sem.at[0]))
    vectors = jnp.concatenate([d_pooled, query, d_target], axis=0)
    vectors = jnp.concatenate([vectors, jnp.zeros((3 * USERS, LANES - E), F32)], axis=1)
    vectors = jnp.concatenate([vectors, jnp.zeros((LANES - 3 * USERS, LANES), F32)], axis=0).T
    for i in range(3 * USERS):
        cast[i] = jnp.broadcast_to(vectors[0:E, i : i + 1], (E, LANES))

    def slot_grads(c):
        at = pl.ds(pl.multiple_of(c * LANES, LANES), LANES)
        w_c, s_c, n_c, a_c = weight[:, at], dscore[:, at], count[:, at], aimed[:, at]
        halves = []
        for h in range(2):
            acc = jnp.zeros((E, LANES), F32)
            for u in range(USERS):
                row = slice(h * USERS + u, h * USERS + u + 1)
                key_grad = w_c[row] * cast[u] + s_c[row] * cast[USERS + u]
                key_grad = key_grad.astype(BF16).astype(F32)
                acc = acc + n_c[row] * key_grad + a_c[row] * cast[2 * USERS + u]
            halves.append(acc)
        slot_grad[at, :] = jnp.concatenate(halves, axis=0).T

    groups = 4
    members, group_chunks = nt // groups, chunks // groups

    def send_grads(to, landing, first_row, count_of, sems):
        src = slot_grad.at[pl.ds(pl.multiple_of(to * pairs + first_row, 8), count_of)]
        dst = landing.at[pl.ds(pl.multiple_of(me * count_of, 8), count_of)]

        @pl.when(to != me)
        def _():
            send(src, dst, sems, {"table": to})

        @pl.when(to == me)
        def _():
            pltpu.make_async_copy(src, dst, sems[1]).start()

    early = early_rows(pairs)
    late = pairs - early
    for g in (2, 1, 3, 0):
        group = lax.rem(lax.div(me, members) + g, groups)

        @pl.loop(0, group_chunks)
        def _(i):
            slot_grads(group * group_chunks + i)

        @pl.loop(0, members)
        def _(i):
            to = group * members + lax.rem(me + i, members)
            send_grads(to, homed_a, 0, early, (grad_sem.at[0], grad_sem.at[1]))

    @pl.loop(0, nt)
    def _(j):
        send_grads(partner(j), homed_b, early, late, (grad_sem.at[2], grad_sem.at[3]))

    drains.append((homed_a.at[pl.ds(0, (nt - 1) * early)], grad_sem.at[0]))
    drains.append((homed_b.at[pl.ds(0, (nt - 1) * late)], grad_sem.at[2]))
    wait_bytes(weights_z, wz_sem.at[1])
    piece = weights[pl.ds(pl.multiple_of(rep * PIECE, 8), PIECE), :]
    for i in range(nr - 1):
        piece = piece + weights_z[i]
    def add_up(ref, count_of):
        out = ref[0]
        for i in range(1, count_of):
            out = out + ref[i]
        return out

    def send_cores():
        weights_c[core] = piece
        send(weights_c.at[core], weights_c.at[core], (wc_sem.at[0], wc_sem.at[1]), {"table": me + 1 - 2 * core})
        drains.append((weights_c.at[0], wc_sem.at[0]))

    def send_x():
        drains.append((weights_x.at[pl.ds(0, CHIPS_X - 1)], wx_sem.at[0]))
        wait_bytes(weights_c.at[0], wc_sem.at[1])
        weights_x[chip_x] = add_up(weights_c, CORES)

        @pl.loop(1, CHIPS_X)
        def _(i):
            to = lax.rem(chip_x + i, CHIPS_X)
            send(weights_x.at[chip_x], weights_x.at[chip_x], (wx_sem.at[0], wx_sem.at[1]),
                 {"table": (chip_y * CHIPS_X + to) * CORES + core})

    def send_y():
        drains.append((weights_y.at[pl.ds(0, chips_y - 1)], wy_sem.at[0]))
        wait_bytes(weights_x.at[pl.ds(0, CHIPS_X - 1)], wx_sem.at[1])
        weights_y[chip_y] = add_up(weights_x, CHIPS_X)

        @pl.loop(1, chips_y)
        def _(i):
            to = lax.rem(chip_y + i, chips_y)
            send(weights_y.at[chip_y], weights_y.at[chip_y], (wy_sem.at[0], wy_sem.at[1]),
                 {"table": (to * CHIPS_X + chip_x) * CORES + core})

    def send_weights():
        wait_bytes(weights_y.at[pl.ds(0, chips_y - 1)], wy_sem.at[1])
        total = add_up(weights_y, chips_y)
        for spot in range(row):
            cuts[spot] = total[spot * PIECE // row : (spot + 1) * PIECE // row]
        spread_out[rep] = cuts[lax.rem(me, row)]

        @pl.loop(1, nr)
        def _(i):
            to = lax.rem(rep + i, nr)
            send(spread_out.at[rep], spread_out.at[rep], (ws_sem.at[0], ws_sem.at[1]), {"rep": to})

        drains.append((spread_out.at[pl.ds(0, nr - 1)], ws_sem.at[0]))

    def share_weights():
        wait_bytes(spread_out.at[pl.ds(0, nr - 1)], ws_sem.at[1])
        spot = lax.rem(me, row)
        joined[spot] = spread_out[...]

        @pl.loop(1, row)
        def _(i):
            to = chip_y * row + lax.rem(spot + i, row)
            send(joined.at[spot], joined.at[spot], (wj_sem.at[0], wj_sem.at[1]), {"table": to})

        drains.append((joined.at[pl.ds(0, row - 1)], wj_sem.at[0]))

    def own(dest, k):
        at = k * nr + dest
        if k == 0:
            rows_of = homed_a[pl.ds(at, nt, stride=early), :]
        else:
            ahead = at < early
            in_a = homed_a[pl.ds(jnp.minimum(at, early - 1), nt, stride=early), :]
            in_b = homed_b[pl.ds(jnp.maximum(at - early, 0), nt, stride=late), :]
            rows_of = jnp.where(ahead, in_a, in_b)
        here = bf16_dot(onehot[at], jnp.concatenate(split3(rows_of), axis=1))
        here = here[:, 0:LANES] + here[:, LANES : 2 * LANES] + here[:, 2 * LANES : 3 * LANES]
        return jnp.where(low_half, here[0:E], here[E : 2 * E])

    plan = [
        (0, 6, 2, ()), (1, 5, 1, ()), (2, -5, -1, ()), (3, 3, 1, ()), (4, -3, -1, ()), (5, 1, 1, ()), (6, -1, -1, ()),
        (7, 4, 2, (0, 1)), (8, -4, -2, (2,)), (9, 2, 2, (7, 3)), (10, -2, -2, (8, 4)), (None, 0, 0, (5, 6, 9, 10)),
    ]
    sign = (1, -1)

    def sum_step(k, first_item, last_item):
        for slot, far, hop, terms in plan[first_item:last_item]:
            value = held[k].pop(0) if held[k] else own(at_rep(sign[k] * far), k)
            for term in terms:
                wait_bytes(got.at[term, k], rs_recv.at[term, k])
                value = value + got[term, k]
            if slot is None:
                return value
            sums[slot, k] = value
            send(sums.at[slot, k], got.at[slot, k], (rs_send.at[slot, k], rs_recv.at[slot, k]), {"rep": at_rep(sign[k] * hop)})
            drains.append((sums.at[slot, k], rs_send.at[slot, k]))

    held = ([], [])

    def adagrad(k, value):
        turned = jnp.concatenate([value, jnp.zeros_like(value)], axis=0).T
        grads = jnp.where(low_half, turned[0:E], pltpu.roll(turned[E : 2 * E], E, 1))
        at = rep * per_rep + k
        new_accum = accum[at] + jnp.sum(grads * grads, axis=0, keepdims=True) * (1.0 / E)
        old = items[:, pl.ds(pl.multiple_of(at * LANES, LANES), LANES)]
        share[rep, k, 0:E, :] = old - LEARN_RATE * grads / jnp.sqrt(new_accum)
        share[rep, k, E : E + 8, :] = jnp.broadcast_to(new_accum, (8, LANES))

    def place(r, k):
        at = r * per_rep + k
        out_rows[:, pl.ds(pl.multiple_of(at * LANES, LANES), LANES)] = share[r, k, 0:E, :]
        out_accum[at] = share[r, k, E : E + 1, :]

    def share_step(k, stage):
        for reach, way in ((6, sign[k]), (5, -sign[k])):
            side = 0 if reach == 6 else 6
            part = share.at[at_rep(-way * 2 * stage), k]
            if stage:
                wait_bytes(part, ag_recv.at[side + 2 * stage - 1, k])
            for hop in (2, 1):
                distance = 2 * stage + hop
                if distance <= reach:
                    at = side + distance - 1
                    send(part, part, (ag_send.at[at, k], ag_recv.at[at, k]), {"rep": at_rep(way * hop)})
                    drains.append((part, ag_send.at[at, k]))

    def place_step(k, distances):
        for distance, side in distances:
            way = sign[k] if side == 0 else -sign[k]
            source = at_rep(-way * distance)
            if distance % 2 or distance == 6:
                wait_bytes(share.at[source, k], ag_recv.at[side + distance - 1, k])
            place(source, k)

    send_cores()
    wait_bytes(homed_a, grad_sem.at[1])
    sum_step(0, 0, 7)
    sum_step(0, 7, 9)
    wait_bytes(homed_b, grad_sem.at[3])
    sum_step(1, 0, 7)
    send_x()
    sum_step(0, 9, 11)
    sum_step(1, 7, 9)
    send_y()
    adagrad(0, sum_step(0, 11, 12))
    share_step(0, 0)
    sum_step(1, 9, 11)
    send_weights()
    place(rep, 0)
    share_step(0, 1)
    adagrad(1, sum_step(1, 11, 12))
    share_step(1, 0)
    share_weights()
    place(rep, 1)
    place_step(0, ((1, 0), (1, 6), (2, 0), (2, 6)))
    share_step(0, 2)
    share_step(1, 1)
    place_step(0, ((3, 0), (3, 6), (4, 0), (4, 6)))
    place_step(1, ((1, 0), (1, 6), (2, 0), (2, 6)))
    share_step(1, 2)
    place_step(0, ((5, 0), (5, 6), (6, 0)))
    place_step(1, ((3, 0), (3, 6), (4, 0), (4, 6)))
    wait_bytes(joined.at[pl.ds(0, row - 1)], wj_sem.at[1])
    for spot in range(row):
        for r in range(nr):
            at = r * PIECE + spot * (PIECE // row)
            whole[at : at + PIECE // row, :] = joined[spot, r]
    flat = whole[...]
    out_hidden[...] = flat[:, 0:HID]
    second = flat[:, LANES : 2 * LANES]
    lane_e = iota((E, LANES), 1)
    query_grad = jnp.where(lane_e < room, pltpu.roll(second[0:E], room, 1), pltpu.roll(second[E : 2 * E], LANES - spare + room, 1))
    out_query[...] = query_grad[:, 0:E]
    tail = second[2 * E : 2 * E + 8]
    lane_1 = iota((1, LANES), 1)

    def turn(row, by):
        return pltpu.roll(tail, by, 1)[row : row + 1]

    row_a = jnp.where(lane_1 < room, turn(0, room), jnp.where(lane_1 < 2 * room, turn(1, 2 * room), turn(2, 2 * room - spare)))
    row_b = jnp.where(lane_1 < room, turn(3, room), turn(4, 2 * room))
    out_logit[:, 0:LANES] = row_a
    out_logit[:, LANES:HID] = row_b[:, 0 : HID - LANES]

    place_step(1, ((5, 0), (5, 6), (6, 0)))

    for ref, sem in drains:
        wait_bytes(ref, sem)


def finish(count_of, *refs):
    sources, results, held = (refs[i * count_of : (i + 1) * count_of] for i in range(3))
    sem = refs[-1]
    inward = [pltpu.make_async_copy(sources[i], held[i], sem.at[0, i]) for i in range(count_of)]
    outward = [pltpu.make_async_copy(held[i], results[i], sem.at[1, i]) for i in range(count_of)]
    for copy in inward:
        copy.start()
    for copy_in, copy_out in zip(inward, outward):
        copy_in.wait()
        copy_out.start()
    for copy in outward:
        copy.wait()


def local(
    nt, nr, item_rows, row_accum, w_query, w_hidden, w_logit, wanted_rows, behaviour_slots,
    target_slots, seq_lengths, clicks, fake_flags,
):
    rows = item_rows.shape[0]
    capacity = wanted_rows.shape[2]
    pairs = capacity // 2
    columns = nt * pairs
    seq = behaviour_slots.shape[1]
    per_rep = pairs // nr
    vmem = pl.BlockSpec(memory_space=pltpu.VMEM)
    hbm = pl.BlockSpec(memory_space=pltpu.HBM)
    dma = pltpu.SemaphoreType.DMA
    wide = 2 * LANES
    row = CORES * CHIPS_X
    scratch = [
        pltpu.VMEM((E, rows), F32),
        pltpu.VMEM((rows // LANES, 1, LANES), F32),
        pltpu.VMEM((E, E), F32),
        pltpu.VMEM((3 * E, HID), F32),
        pltpu.VMEM((1, HID), F32),
        pltpu.VMEM((capacity, nt), jnp.int32),
        pltpu.VMEM((USERS, seq), jnp.int32),
        pltpu.SMEM((USERS,), jnp.int32),
        pltpu.SMEM((USERS,), jnp.int32),
        pltpu.SMEM((USERS,), jnp.int32),
        pltpu.SMEM((USERS,), jnp.int32),
        pltpu.VMEM((3 * LANES, rows), BF16),
        pltpu.VMEM((nt, 1, LANES), jnp.int32),
        pltpu.VMEM((nt, 1, LANES), jnp.int32),
        pltpu.VMEM((pairs, LANES, nt), BF16),
        pltpu.VMEM((columns, LANES), F32),
        pltpu.VMEM((columns, LANES), F32),
        pltpu.VMEM((LANES, columns), F32),
        pltpu.VMEM((2 * USERS, columns), F32),
        pltpu.VMEM((2 * USERS, columns), F32),
        pltpu.VMEM((USERS, 1, seq), jnp.int32),
        pltpu.VMEM((USERS, 1, seq), jnp.int32),
        pltpu.VMEM((2 * USERS, columns), F32),
        pltpu.VMEM((2 * USERS, columns), F32),
        pltpu.VMEM((3 * USERS, E, LANES), F32),
        pltpu.VMEM((columns, LANES), F32),
        pltpu.VMEM((nt * early_rows(pairs), LANES), F32),
        pltpu.VMEM((nt * (pairs - early_rows(pairs)), LANES), F32),
        pltpu.VMEM((LANES, 1, LANES), jnp.int32),
        pltpu.VMEM((USERS, 2 * columns // LANES, LANES), F32),
        pltpu.VMEM((nr - 1, per_rep, E, LANES), F32),
        pltpu.VMEM((nr - 1, per_rep, E, LANES), F32),
        pltpu.VMEM((nr * PIECE, wide), F32),
        pltpu.VMEM((nr - 1, PIECE, wide), F32),
        pltpu.VMEM((CORES, PIECE, wide), F32),
        pltpu.VMEM((CHIPS_X, PIECE, wide), F32),
        pltpu.VMEM((nt // (CORES * CHIPS_X), PIECE, wide), F32),
        pltpu.VMEM((row, PIECE // row, wide), F32),
        pltpu.VMEM((nr, PIECE // row, wide), F32),
        pltpu.VMEM((row, nr, PIECE // row, wide), F32),
        pltpu.VMEM((nr * PIECE, wide), F32),
        pltpu.VMEM((nr, per_rep, E + 8, LANES), F32),
        dma((11,)), dma((2,)), dma((2,)), dma((4,)), dma((2,)), dma((2,)), dma((2,)), dma((2,)), dma((2,)), dma((2,)),
        dma((nr - 1, per_rep)), dma((nr - 1, per_rep)), dma((nr - 1, 2)), dma((nr - 1, 2)),
    ]
    results = pl.pallas_call(
        functools.partial(kernel, nt, nr, capacity),
        out_shape=(
            jax.ShapeDtypeStruct((E, rows), F32),
            jax.ShapeDtypeStruct((rows // LANES, 1, LANES), F32),
            jax.ShapeDtypeStruct((E, E), F32),
            jax.ShapeDtypeStruct((3 * E, HID), F32),
            jax.ShapeDtypeStruct((1, HID), F32),
        ),
        in_specs=[hbm] * 11,
        out_specs=[vmem] * 5,
        scratch_shapes=scratch,
        compiler_params=pltpu.CompilerParams(
            collective_id=0, has_side_effects=True, vmem_limit_bytes=VMEM
        ),
    )(
        item_rows.T,
        row_accum.reshape(rows // LANES, 1, LANES),
        w_query,
        w_hidden,
        w_logit.reshape(1, HID),
        wanted_rows[0].T,
        behaviour_slots,
        target_slots,
        seq_lengths,
        clicks,
        fake_flags,
    )
    new_rows, new_accum, grad_query, grad_hidden, grad_logit = pl.pallas_call(
        functools.partial(finish, 5),
        out_shape=[jax.ShapeDtypeStruct(result.shape, result.dtype) for result in results],
        in_specs=[hbm] * 5,
        out_specs=[hbm] * 5,
        scratch_shapes=[pltpu.VMEM(result.shape, result.dtype) for result in results] + [dma((2, 5))],
        compiler_params=pltpu.CompilerParams(vmem_limit_bytes=VMEM),
    )(*results)
    return (new_rows.T, new_accum.reshape(rows), grad_query, grad_hidden, grad_logit.reshape(HID))


def solution(mesh):
    in_specs = (
        P("table", None),
        P("table"),
        P(),
        P(),
        P(),
        P(("table", "rep"), None, None),
        P(("table", "rep"), None),
        P(("table", "rep")),
        P(("table", "rep")),
        P(("table", "rep")),
        P(("table", "rep")),
    )
    out_specs = (P("table", None), P("table"), P(), P(), P())
    return jax.shard_map(
        functools.partial(local, mesh.shape["table"], mesh.shape["rep"]),
        mesh=mesh, in_specs=in_specs, out_specs=out_specs, check_vma=False,
    )
```

time: 135 us -> 107 us (0.79)
  the two profiles are of different devices: /device:TPU:16 before, /device:TPU:4 now
where the time goes in v2:
time: 107 us
  Pallas kernels  107 us (100%)
    pallas_call x1, Pallas kernels, local(): pl.pallas_call(functools.partial(kernel, nt, nr, capacity), out_shape=(ja...  104 us
    pallas_call x1, Pallas kernels, local(): pl.pallas_call(functools.partial(finish, 5), out_shape=[jax.ShapeDtypeStr...  2.17 us

profile of v2, /device:TPU:4, one launch (start us, length us, event | category | flops | bytes accessed | tf_op | source)
XLA Modules:
  0.0 107.2 jit_solution(9059994147890682756)
XLA Ops:
  0.6 104.4 %shard_map.146 = (f32[64,3072]{1,0:T(8,128)}, f32[24,1,128]{2,1,0:T(1,128)}, f32[64,64]{1,0:T(8,128)}, f32[192,200]{1,0:T(8,128)}, f32[1,200]{1,0:T(1,128)}) custom-call(f32[64,3072]{1,0:T(8,128)} %bitcast.9, f32[24,1,128]{2,1,0:T(1,128)} %bitcast.11, f32[64,64]{1,0:T(8,128)} %w_query_hbm.1, f32[192,200]{1,0:T(8,128)} %w_hidden_hbm.1, f32[1,200]{1,0:T(1,128)} %bitcast.12, ...), custom_call_target="tpu_custom_call" | custom-call | tf_op jit(solution)/shard_map/pallas_call | solution.py:601
  105.0 2.2 %shard_map.147 = (f32[64,3072]{1,0:T(8,128)}, f32[24,1,128]{2,1,0:T(1,128)}, f32[64,64]{1,0:T(8,128)}, f32[192,200]{1,0:T(8,128)}, f32[1,200]{1,0:T(1,128)}) custom-call(f32[64,3072]{1,0:T(8,128)} %get-tuple-element.15.refs_0_, f32[24,1,128]{2,1,0:T(1,128)} %get-tuple-element.16.refs_1_, f32[64,64]{1,0:T(8,128)} %get-tuple-element.17.refs_2_, ...), custom_call_target="tpu_custom_call" | custom-call | tf_op jit(solution)/shard_map/pallas_call | solution.py:629

commit v3 on v2

--- a/solution.py
+++ b/solution.py
@@ -70,9 +70,9 @@
     targets_hbm, lengths_hbm, clicks_hbm, flags_hbm,
     out_rows, out_accum, out_query, out_hidden, out_logit,
     items, accum, w_query, w_hidden, w_logit, want, slots, targets, lengths, clicks, flags,
-    parts, asked_out, asked, onehot, looked, fetched, fetched_t, count, aimed, code_hi, code_lo,
+    parts, asked_out, asked, onehot, looked, fetched, keys, count, aimed, code_hi, code_lo,
     weight, dscore, cast, slot_grad, homed_a, homed_b, index_t, named, sums, got,
-    weights, weights_z, weights_c, weights_x, weights_y, cuts, spread_out, joined, whole, share,
+    weights, weights_z, weights_c, weights_x, weights_y, cuts, spread_out, joined, whole, accums, share,
     in_sem, ask_sem, row_sem, grad_sem, wz_sem, wc_sem, wx_sem, wy_sem, ws_sem, wj_sem, rs_send, rs_recv, ag_send, ag_recv,
 ):
     me, rep = lax.axis_index("table"), lax.axis_index("rep")
@@ -155,30 +155,6 @@
         parts[p * LANES : p * LANES + E, :] = jnp.where(wide_low, part, 0.0).astype(BF16)
         parts[p * LANES + E : (p + 1) * LANES, :] = jnp.where(wide_low, 0.0, part).astype(BF16)
 
-    seq = slots.shape[1]
-    place, half = place_of(slots[...], capacity)
-    chunks = columns // LANES
-    valid = iota((USERS, seq), 1) < column(lengths)
-    code_hi[...] = jnp.where(valid, half * chunks + lax.shift_right_logical(place, 7), -1).reshape(USERS, 1, seq)
-    code_lo[...] = (place & (LANES - 1)).reshape(USERS, 1, seq)
-
-    @pl.loop(0, USERS)
-    def _(user):
-        hi = (iota((2 * chunks, seq), 0) == code_hi[user]).astype(F32).astype(BF16)
-        lo = (iota((LANES, seq), 0) == code_lo[user]).astype(F32).astype(BF16)
-        named[user] = bf16_dot(hi, lo, ((1,), (1,)))
-
-    for h in range(2):
-        for c in range(chunks):
-            count[h * USERS : (h + 1) * USERS, c * LANES : (c + 1) * LANES] = named[:, h * chunks + c, :]
-
-    target_place, target_half = place_of(column(targets), capacity)
-    lane = iota((USERS, columns), 1)
-    hit = lane == target_place
-    for h in range(2):
-        aimed[h * USERS : (h + 1) * USERS, :] = (hit & (target_half == h)).astype(F32)
-    weights[:, LANES : 2 * LANES] = jnp.zeros((3 * E, LANES), F32)
-
     wait_bytes(asked, ask_sem.at[1])
 
     asked_t = jnp.concatenate([asked[...].reshape(nt, LANES), jnp.zeros((LANES - nt, LANES), jnp.int32)], axis=0).T
@@ -196,20 +172,74 @@
         found = found[0:LANES] + found[LANES : 2 * LANES] + found[2 * LANES : 3 * LANES]
         looked[pl.ds(p, nt, stride=pairs), :] = found.T
 
-    pltpu.make_async_copy(looked.at[block(me)], fetched.at[block(me)], row_sem.at[1]).start()
-
-    @pl.loop(0, nt - 1)
-    def _(j):
-        to = partner(j)
-        send(looked.at[block(to)], fetched.at[block(me)], (row_sem.at[0], row_sem.at[1]), {"table": to})
-
-    drains.append((looked.at[pl.ds(0, (nt - 1) * pairs)], row_sem.at[0]))
-    wait_bytes(fetched, row_sem.at[1])
-
-    @pl.loop(0, chunks)
-    def _(c):
-        at = pl.ds(pl.multiple_of(c * LANES, LANES), LANES)
-        fetched_t[:, at] = fetched[at, :].T
+    groups = 4
+    members, group_chunks = nt // groups, columns // LANES // groups
+    my_group = lax.div(me, members)
+
+    def send_rows(ahead, i):
+        to = lax.rem(my_group + ahead, groups) * members + lax.rem(me + i, members)
+        send(looked.at[block(to)], fetched.at[block(me)], (row_sem.at[4], row_sem.at[ahead]), {"table": to})
+
+    pltpu.make_async_copy(looked.at[block(me)], fetched.at[block(me)], row_sem.at[0]).start()
+
+    @pl.loop(0, members)
+    def _(i):
+        send_rows(2, i)
+
+    @pl.loop(0, members)
+    def _(i):
+        send_rows(1, i)
+        send_rows(3, i)
+
+    @pl.loop(1, members)
+    def _(i):
+        send_rows(0, i)
+
+    drains.append((looked.at[pl.ds(0, (nt - 1) * pairs)], row_sem.at[4]))
+    seq = slots.shape[1]
+    place, half = place_of(slots[...], capacity)
+    chunks = columns // LANES
+    valid = iota((USERS, seq), 1) < column(lengths)
+    code_hi[...] = jnp.where(valid, half * chunks + lax.shift_right_logical(place, 7), -1).reshape(USERS, 1, seq)
+    code_lo[...] = (place & (LANES - 1)).reshape(USERS, 1, seq)
+
+    @pl.loop(0, USERS)
+    def _(user):
+        hi = (iota((2 * chunks, seq), 0) == code_hi[user]).astype(F32).astype(BF16)
+        lo = (iota((LANES, seq), 0) == code_lo[user]).astype(F32).astype(BF16)
+        named[user] = bf16_dot(hi, lo, ((1,), (1,)))
+
+    for h in range(2):
+        for c in range(chunks):
+            count[h * USERS : (h + 1) * USERS, c * LANES : (c + 1) * LANES] = named[:, h * chunks + c, :]
+
+    target_place, target_half = place_of(column(targets), capacity)
+    lane = iota((USERS, columns), 1)
+    hit = lane == target_place
+    for h in range(2):
+        aimed[h * USERS : (h + 1) * USERS, :] = (hit & (target_half == h)).astype(F32)
+    weights[:, LANES : 2 * LANES] = jnp.zeros((3 * E, LANES), F32)
+    accums[...] = jnp.zeros_like(accums)
+
+    found = jnp.zeros((2 * USERS, LANES), F32)
+    for ahead in (2, 1, 3, 0):
+        span = group_chunks * LANES
+        at = pl.ds(pl.multiple_of(lax.rem(my_group + groups - ahead, groups) * span, LANES), span)
+        wait_bytes(fetched.at[at], row_sem.at[ahead])
+        picks = aimed[:, at].astype(BF16)
+        for p, part in enumerate(split3(fetched[at, :])):
+            keys[p, at, :] = part
+            found = found + bf16_dot(picks, part)
+
+    def stacked_dot(x, contract):
+        high, middle, low = split3(x)
+        n = x.shape[0]
+        first = bf16_dot(jnp.concatenate([high, middle, low], axis=0), keys[0], contract)
+        second = bf16_dot(jnp.concatenate([high, middle], axis=0), keys[1], contract)
+        third = bf16_dot(high, keys[2], contract)
+        return first[0:n] + ((first[n : 2 * n] + second[0:n]) + (first[2 * n : 3 * n] + second[n : 2 * n] + third))
+
+    along, across = ((1,), (0,)), ((1,), (1,))
 
     def fold(x):
         return x[0:USERS, 0:E] + x[USERS : 2 * USERS, E : 2 * E]
@@ -223,10 +253,9 @@
     def both(x):
         return jnp.concatenate([x, x], axis=0)
 
-    keys = fetched[...]
-    target = fold(exact_dot(aimed[...], keys))
+    target = fold(found)
     query = exact_dot(target, w_query[...]) * E ** (-0.5)
-    scores = exact_dot(spread(query), fetched_t[...])
+    scores = stacked_dot(spread(query), across)
     times = count[...]
     present = times > 0.0
     scores = jnp.where(present, scores, -1e30)
@@ -237,7 +266,7 @@
     total = both(total[0:USERS] + total[USERS : 2 * USERS])
     attention = raised / total
     weight[...] = attention
-    pooled = fold(exact_dot(attention * times, keys))
+    pooled = fold(stacked_dot(attention * times, along))
     features = jnp.concatenate([pooled, target, pooled * target], axis=1)
     before = exact_dot(features, w_hidden[...])
     gate = sigmoid(before)
@@ -253,11 +282,11 @@
     d_cross = d_features[:, 2 * E : 3 * E]
     d_pooled = d_features[:, 0:E] + d_cross * target
     d_target = d_features[:, E : 2 * E] + d_cross * pooled
-    pull = exact_dot(spread(d_pooled), fetched_t[...])
+    pull = stacked_dot(spread(d_pooled), across)
     shift = jnp.sum(pooled * d_pooled, axis=1, keepdims=True)
     d_scores = attention * (pull - both(shift))
     dscore[...] = d_scores
-    d_query = fold(exact_dot(d_scores * times, keys)) * E ** (-0.5)
+    d_query = fold(stacked_dot(d_scores * times, along)) * E ** (-0.5)
     d_target = d_target + exact_dot(d_query, w_query[...], ((1,), (1,)))
     d_w_query = exact_dot(target.T, d_query)
     spare = HID - LANES
@@ -301,9 +330,6 @@
             halves.append(acc)
         slot_grad[at, :] = jnp.concatenate(halves, axis=0).T
 
-    groups = 4
-    members, group_chunks = nt // groups, chunks // groups
-
     def send_grads(to, landing, first_row, count_of, sems):
         src = slot_grad.at[pl.ds(pl.multiple_of(to * pairs + first_row, 8), count_of)]
         dst = landing.at[pl.ds(pl.multiple_of(me * count_of, 8), count_of)]
@@ -319,16 +345,16 @@
     early = early_rows(pairs)
     late = pairs - early
     for g in (2, 1, 3, 0):
-        group = lax.rem(lax.div(me, members) + g, groups)
-
-        @pl.loop(0, group_chunks)
-        def _(i):
+        group = lax.rem(my_group + g, groups)
+
+        for i in range(group_chunks):
             slot_grads(group * group_chunks + i)
-
-        @pl.loop(0, members)
-        def _(i):
-            to = group * members + lax.rem(me + i, members)
-            send_grads(to, homed_a, 0, early, (grad_sem.at[0], grad_sem.at[1]))
+            low, high = i * LANES // pairs, (i + 1) * LANES // pairs
+
+            @pl.loop(0, high - low)
+            def _(m):
+                to = group * members + low + lax.rem(me + m, high - low)
+                send_grads(to, homed_a, 0, early, (grad_sem.at[0], grad_sem.at[1]))
 
     @pl.loop(0, nt)
     def _(j):
@@ -412,25 +438,43 @@
         here = here[:, 0:LANES] + here[:, LANES : 2 * LANES] + here[:, 2 * LANES : 3 * LANES]
         return jnp.where(low_half, here[0:E], here[E : 2 * E])
 
-    plan = [
-        (0, 6, 2, ()), (1, 5, 1, ()), (2, -5, -1, ()), (3, 3, 1, ()), (4, -3, -1, ()), (5, 1, 1, ()), (6, -1, -1, ()),
-        (7, 4, 2, (0, 1)), (8, -4, -2, (2,)), (9, 2, 2, (7, 3)), (10, -2, -2, (8, 4)), (None, 0, 0, (5, 6, 9, 10)),
-    ]
+    strides = (2, 2)
     sign = (1, -1)
-
-    def sum_step(k, first_item, last_item):
-        for slot, far, hop, terms in plan[first_item:last_item]:
-            value = held[k].pop(0) if held[k] else own(at_rep(sign[k] * far), k)
-            for term in terms:
-                wait_bytes(got.at[term, k], rs_recv.at[term, k])
-                value = value + got[term, k]
-            if slot is None:
-                return value
-            sums[slot, k] = value
-            send(sums.at[slot, k], got.at[slot, k], (rs_send.at[slot, k], rs_recv.at[slot, k]), {"rep": at_rep(sign[k] * hop)})
-            drains.append((sums.at[slot, k], rs_send.at[slot, k]))
-
-    held = ([], [])
+    reaches = ((nr // 2, 1), (nr - 1 - nr // 2, -1))
+
+    def plan_of(stride):
+        stages = {}
+        slot = {}
+        for reach, way in reaches:
+            for distance in range(reach, 0, -1):
+                level = distance // stride if distance % stride == 0 and distance < reach else None
+                slot[distance * way] = len(slot)
+                terms = () if level is None else tuple(
+                    slot[way * d] for d in range(distance + 1, min(distance + stride, reach) + 1)
+                )
+                hop = (distance - 1) % stride + 1
+                stages.setdefault(level, []).append((slot[distance * way], distance * way, hop * way, terms))
+        top = max(level for level in stages if level is not None)
+        leaves = sorted(stages[None], key=lambda item: -abs(item[1]))
+        last = tuple(slot[way * d] for reach, way in reaches for d in range(1, stride + 1))
+        return [leaves] + [stages[level] for level in range(top, 0, -1)] + [[(None, 0, 0, last)]]
+
+    plans = [plan_of(stride) for stride in strides]
+
+    def sum_stage(k, stage):
+        items_of = plans[k][stage]
+        for start in range(0, len(items_of), 3):
+            batch = items_of[start : start + 3]
+            values = [own(at_rep(sign[k] * far), k) for _, far, _, _ in batch]
+            for value, (slot, _, hop, terms) in zip(values, batch):
+                for term in terms:
+                    wait_bytes(got.at[term, k], rs_recv.at[term, k])
+                    value = value + got[term, k]
+                if slot is None:
+                    return value
+                sums[slot, k] = value
+                send(sums.at[slot, k], got.at[slot, k], (rs_send.at[slot, k], rs_recv.at[slot, k]), {"rep": at_rep(sign[k] * hop)})
+                drains.append((sums.at[slot, k], rs_send.at[slot, k]))
 
     def adagrad(k, value):
         turned = jnp.concatenate([value, jnp.zeros_like(value)], axis=0).T
@@ -439,62 +483,74 @@
         new_accum = accum[at] + jnp.sum(grads * grads, axis=0, keepdims=True) * (1.0 / E)
         old = items[:, pl.ds(pl.multiple_of(at * LANES, LANES), LANES)]
         share[rep, k, 0:E, :] = old - LEARN_RATE * grads / jnp.sqrt(new_accum)
-        share[rep, k, E : E + 8, :] = jnp.broadcast_to(new_accum, (8, LANES))
+        accums[k : k + 1, :] = new_accum
+        if k == per_rep - 1:
+            share[rep, k, E : E + 8, :] = accums[...]
 
     def place(r, k):
         at = r * per_rep + k
         out_rows[:, pl.ds(pl.multiple_of(at * LANES, LANES), LANES)] = share[r, k, 0:E, :]
-        out_accum[at] = share[r, k, E : E + 1, :]
-
-    def share_step(k, stage):
-        for reach, way in ((6, sign[k]), (5, -sign[k])):
-            side = 0 if reach == 6 else 6
-            part = share.at[at_rep(-way * 2 * stage), k]
-            if stage:
-                wait_bytes(part, ag_recv.at[side + 2 * stage - 1, k])
-            for hop in (2, 1):
-                distance = 2 * stage + hop
+        if k == per_rep - 1:
+            for i in range(per_rep):
+                out_accum[r * per_rep + i] = share[r, k, E + i : E + i + 1, :]
+
+    def block_of(r, k):
+        return share.at[r, k, pl.ds(0, E + 8 * (k == per_rep - 1))]
+
+    def share_stage(k, stage):
+        stride = strides[k]
+        for reach, way in reaches:
+            side = 0 if way == 1 else nr // 2
+            part = block_of(at_rep(-sign[k] * way * stride * stage), k)
+            if stage and stride * stage < reach:
+                wait_bytes(part, ag_recv.at[side + stride * stage - 1, k])
+            for hop in range(stride, 0, -1):
+                distance = stride * stage + hop
                 if distance <= reach:
                     at = side + distance - 1
-                    send(part, part, (ag_send.at[at, k], ag_recv.at[at, k]), {"rep": at_rep(way * hop)})
+                    send(part, part, (ag_send.at[at, k], ag_recv.at[at, k]), {"rep": at_rep(sign[k] * way * hop)})
                     drains.append((part, ag_send.at[at, k]))
 
-    def place_step(k, distances):
-        for distance, side in distances:
-            way = sign[k] if side == 0 else -sign[k]
-            source = at_rep(-way * distance)
-            if distance % 2 or distance == 6:
-                wait_bytes(share.at[source, k], ag_recv.at[side + distance - 1, k])
-            place(source, k)
+    def place_stage(k, stage):
+        stride = strides[k]
+        for hop in range(1, stride + 1):
+            for reach, way in reaches:
+                side = 0 if way == 1 else nr // 2
+                distance = stride * stage + hop
+                if distance <= reach:
+                    source = at_rep(-sign[k] * way * distance)
+                    if distance % stride or distance == reach:
+                        wait_bytes(block_of(source, k), ag_recv.at[side + distance - 1, k])
+                    place(source, k)
 
     send_cores()
     wait_bytes(homed_a, grad_sem.at[1])
-    sum_step(0, 0, 7)
-    sum_step(0, 7, 9)
+    sum_stage(0, 0)
+    sum_stage(0, 1)
     wait_bytes(homed_b, grad_sem.at[3])
-    sum_step(1, 0, 7)
+    sum_stage(1, 0)
     send_x()
-    sum_step(0, 9, 11)
-    sum_step(1, 7, 9)
+    sum_stage(0, 2)
+    sum_stage(1, 1)
     send_y()
-    adagrad(0, sum_step(0, 11, 12))
-    share_step(0, 0)
-    sum_step(1, 9, 11)
+    adagrad(0, sum_stage(0, 3))
+    share_stage(0, 0)
+    sum_stage(1, 2)
     send_weights()
     place(rep, 0)
-    share_step(0, 1)
-    adagrad(1, sum_step(1, 11, 12))
-    share_step(1, 0)
+    share_stage(0, 1)
+    adagrad(1, sum_stage(1, 3))
+    share_stage(1, 0)
     share_weights()
     place(rep, 1)
-    place_step(0, ((1, 0), (1, 6), (2, 0), (2, 6)))
-    share_step(0, 2)
-    share_step(1, 1)
-    place_step(0, ((3, 0), (3, 6), (4, 0), (4, 6)))
-    place_step(1, ((1, 0), (1, 6), (2, 0), (2, 6)))
-    share_step(1, 2)
-    place_step(0, ((5, 0), (5, 6), (6, 0)))
-    place_step(1, ((3, 0), (3, 6), (4, 0), (4, 6)))
+    share_stage(0, 2)
+    place_stage(0, 0)
+    share_stage(1, 1)
+    place_stage(0, 1)
+    place_stage(1, 0)
+    share_stage(1, 2)
+    place_stage(0, 2)
+    place_stage(1, 1)
     wait_bytes(joined.at[pl.ds(0, row - 1)], wj_sem.at[1])
     for spot in range(row):
         for r in range(nr):
@@ -517,23 +573,18 @@
     out_logit[:, 0:LANES] = row_a
     out_logit[:, LANES:HID] = row_b[:, 0 : HID - LANES]
 
-    place_step(1, ((5, 0), (5, 6), (6, 0)))
+    place_stage(1, 2)
 
     for ref, sem in drains:
         wait_bytes(ref, sem)
 
 
 def finish(count_of, *refs):
-    sources, results, held = (refs[i * count_of : (i + 1) * count_of] for i in range(3))
     sem = refs[-1]
-    inward = [pltpu.make_async_copy(sources[i], held[i], sem.at[0, i]) for i in range(count_of)]
-    outward = [pltpu.make_async_copy(held[i], results[i], sem.at[1, i]) for i in range(count_of)]
-    for copy in inward:
+    copies = [pltpu.make_async_copy(refs[i], refs[count_of + i], sem.at[i]) for i in range(count_of)]
+    for copy in copies:
         copy.start()
-    for copy_in, copy_out in zip(inward, outward):
-        copy_in.wait()
-        copy_out.start()
-    for copy in outward:
+    for copy in copies:
         copy.wait()
 
 
@@ -548,6 +599,10 @@
     seq = behaviour_slots.shape[1]
     per_rep = pairs // nr
     vmem = pl.BlockSpec(memory_space=pltpu.VMEM)
+
+    def in_hbm(x):
+        return pltpu.with_memory_space_constraint(x, pltpu.HBM)
+
     hbm = pl.BlockSpec(memory_space=pltpu.HBM)
     dma = pltpu.SemaphoreType.DMA
     wide = 2 * LANES
@@ -570,7 +625,7 @@
         pltpu.VMEM((pairs, LANES, nt), BF16),
         pltpu.VMEM((columns, LANES), F32),
         pltpu.VMEM((columns, LANES), F32),
-        pltpu.VMEM((LANES, columns), F32),
+        pltpu.VMEM((3, columns, LANES), BF16),
         pltpu.VMEM((2 * USERS, columns), F32),
         pltpu.VMEM((2 * USERS, columns), F32),
         pltpu.VMEM((USERS, 1, seq), jnp.int32),
@@ -594,18 +649,19 @@
         pltpu.VMEM((nr, PIECE // row, wide), F32),
         pltpu.VMEM((row, nr, PIECE // row, wide), F32),
         pltpu.VMEM((nr * PIECE, wide), F32),
+        pltpu.VMEM((8, LANES), F32),
         pltpu.VMEM((nr, per_rep, E + 8, LANES), F32),
-        dma((11,)), dma((2,)), dma((2,)), dma((4,)), dma((2,)), dma((2,)), dma((2,)), dma((2,)), dma((2,)), dma((2,)),
+        dma((11,)), dma((2,)), dma((5,)), dma((4,)), dma((2,)), dma((2,)), dma((2,)), dma((2,)), dma((2,)), dma((2,)),
         dma((nr - 1, per_rep)), dma((nr - 1, per_rep)), dma((nr - 1, 2)), dma((nr - 1, 2)),
     ]
     results = pl.pallas_call(
         functools.partial(kernel, nt, nr, capacity),
         out_shape=(
-            jax.ShapeDtypeStruct((E, rows), F32),
-            jax.ShapeDtypeStruct((rows // LANES, 1, LANES), F32),
-            jax.ShapeDtypeStruct((E, E), F32),
-            jax.ShapeDtypeStruct((3 * E, HID), F32),
-            jax.ShapeDtypeStruct((1, HID), F32),
+            pltpu.VMEM((E, rows), F32),
+            pltpu.VMEM((rows // LANES, 1, LANES), F32),
+            pltpu.VMEM((E, E), F32),
+            pltpu.VMEM((3 * E, HID), F32),
+            pltpu.VMEM((1, HID), F32),
         ),
         in_specs=[hbm] * 11,
         out_specs=[vmem] * 5,
@@ -614,26 +670,26 @@
             collective_id=0, has_side_effects=True, vmem_limit_bytes=VMEM
         ),
     )(
-        item_rows.T,
-        row_accum.reshape(rows // LANES, 1, LANES),
-        w_query,
-        w_hidden,
-        w_logit.reshape(1, HID),
-        wanted_rows[0].T,
-        behaviour_slots,
-        target_slots,
-        seq_lengths,
-        clicks,
-        fake_flags,
+        in_hbm(item_rows.T),
+        in_hbm(row_accum.reshape(rows // LANES, 1, LANES)),
+        in_hbm(w_query),
+        in_hbm(w_hidden),
+        in_hbm(w_logit.reshape(1, HID)),
+        in_hbm(wanted_rows[0].T),
+        in_hbm(behaviour_slots),
+        in_hbm(target_slots),
+        in_hbm(seq_lengths),
+        in_hbm(clicks),
+        in_hbm(fake_flags),
     )
     new_rows, new_accum, grad_query, grad_hidden, grad_logit = pl.pallas_call(
         functools.partial(finish, 5),
         out_shape=[jax.ShapeDtypeStruct(result.shape, result.dtype) for result in results],
-        in_specs=[hbm] * 5,
+        in_specs=[vmem] * 5,
         out_specs=[hbm] * 5,
-        scratch_shapes=[pltpu.VMEM(result.shape, result.dtype) for result in results] + [dma((2, 5))],
+        scratch_shapes=[dma((5,))],
         compiler_params=pltpu.CompilerParams(vmem_limit_bytes=VMEM),
-    )(*results)
+    )(*[pltpu.with_memory_space_constraint(result, pltpu.VMEM) for result in results])
     return (new_rows.T, new_accum.reshape(rows), grad_query, grad_hidden, grad_logit.reshape(HID))
 
 

time: 107 us -> 105 us (0.981)
  the two profiles are of different devices: /device:TPU:4 before, /device:TPU:10 now
where the time goes in v3:
time: 105 us
  Pallas kernels  104 us (99%)
    pallas_call x1, Pallas kernels, local(): pl.pallas_call(functools.partial(kernel, nt, nr, capacity), out_shape=(pl...  103 us

profile of v3, /device:TPU:10, one launch (start us, length us, event | category | flops | bytes accessed | tf_op | source)
XLA Modules:
  0.0 105.0 jit_solution(16367293644401223912)
XLA Ops:
  0.6 103.4 %shard_map.146 = (f32[64,3072]{1,0:T(8,128)S(1)}, f32[24,1,128]{2,1,0:T(1,128)S(1)}, f32[64,64]{1,0:T(8,128)S(1)}, f32[192,200]{1,0:T(8,128)S(1)}, f32[1,200]{1,0:T(1,128)S(1)}) custom-call(f32[64,3072]{1,0:T(8,128)} %bitcast.9, f32[24,1,128]{2,1,0:T(1,128)} %bitcast.11, f32[64,64]{1,0:T(8,128)} %w_query_hbm.1, f32[192,200]{1,0:T(8,128)} %w_hidden_hbm.1, ...), custom_call_target="tpu_custom_call" | custom-call | tf_op jit(solution)/shard_map/pallas_call | solution.py:657
  104.0 1.0 shard_map.147

commit v4 on v3

--- a/solution.py
+++ b/solution.py
@@ -439,7 +439,7 @@
         return jnp.where(low_half, here[0:E], here[E : 2 * E])
 
     strides = (2, 2)
-    sign = (1, -1)
+    sign = (1 - 2 * core, 2 * core - 1)
     reaches = ((nr // 2, 1), (nr - 1 - nr // 2, -1))
 
     def plan_of(stride):

time: 105 us -> 104 us (level)
    pallas_call x1, Pallas kernels: 103 us -> 102 us  [local(): pl.pallas_call(functools.partial(kernel, nt, nr, capacity), out_shape=(pl...]
where the time goes in v4:
time: 104 us
  Pallas kernels  103 us (99%)
    pallas_call x1, Pallas kernels, local(): pl.pallas_call(functools.partial(kernel, nt, nr, capacity), out_shape=(pl...  102 us

profile of v4, /device:TPU:10, one launch (start us, length us, event | category | flops | bytes accessed | tf_op | source)
XLA Modules:
  0.0 103.6 jit_solution(265767422079059658)
XLA Ops:
  0.6 101.9 %shard_map.146 = (f32[64,3072]{1,0:T(8,128)S(1)}, f32[24,1,128]{2,1,0:T(1,128)S(1)}, f32[64,64]{1,0:T(8,128)S(1)}, f32[192,200]{1,0:T(8,128)S(1)}, f32[1,200]{1,0:T(1,128)S(1)}) custom-call(f32[64,3072]{1,0:T(8,128)} %bitcast.9, f32[24,1,128]{2,1,0:T(1,128)} %bitcast.11, f32[64,64]{1,0:T(8,128)} %w_query_hbm.1, f32[192,200]{1,0:T(8,128)} %w_hidden_hbm.1, ...), custom_call_target="tpu_custom_call" | custom-call | tf_op jit(solution)/shard_map/pallas_call | solution.py:657
  102.6 1.0 shard_map.147
